TPU v7x, 768 devices: a whole 4x8x12 slice. The times are simulated.
768 devices in a mesh: dp: 384 (over x, y, z), tensor: 2 (over core).
Axes of the slice: x: 4, y: 8, z: 12, core: 2. Of those that a mesh axis runs over, the one named last changes fastest.
Arguments:
- weight: float32 [6144, 9216], P('dp', 'tensor'), may hold values from -6 to 6
- momentum: float32 [6144, 9216], P('dp', 'tensor'), may hold values from -6 to 6
- grad: bfloat16 [6144, 9216], P('dp', 'tensor'), may hold values from -24 to 24
- right_factor: float32 [9216, 128], P('tensor'), may hold values from -0.0625 to 0.0625
Outputs:
- new_weight: float32 [6144, 9216], P('dp', 'tensor')
- new_momentum: float32 [6144, 9216], P('dp', 'tensor')
- new_factor: float32 [9216, 128], P('tensor')
All inputs are finite; a program needn't handle non-finite values.
Results may differ from a plain program's by a relative error of at most 0.00075.
Values sent between devices are 32-bit elements; how exact they have to be, the bound alone decides.
No kernel may reach another device: no remote copies, remote signals or barrier semaphores. Data moves between devices by JAX's collectives and lax.ppermute only.
A program may use at most 32 MiB of HBM per device.

v0:
```python
import math

import jax
import jax.numpy as jnp
from jax import lax
from jax.sharding import PartitionSpec as P

PRECISE = lax.Precision.HIGHEST


def solve_rows(lower_factor, rows):
    return lax.linalg.triangular_solve(
        lower_factor, rows, left_side=False, lower=True, transpose_a=True
    )


def per_device(weight, momentum, grad, right_factor):
    buffer = momentum + grad.astype(jnp.float32)
    left_raw = lax.psum(jnp.dot(buffer, right_factor, precision=PRECISE), "tensor")
    gram_part = jnp.dot(left_raw.T, left_raw, precision=PRECISE)
    gram = lax.psum(gram_part, "dp")
    lower_factor = jnp.linalg.cholesky(gram)
    left = solve_rows(lower_factor, left_raw)
    right = lax.psum(jnp.dot(buffer.T, left, precision=PRECISE), "dp")
    squares = lax.psum(jnp.sum(right * right, axis=0), "tensor")
    new_factor = right * lax.rsqrt(squares + 1e-06)
    new_momentum = buffer - (1.0 - 0.95) * jnp.dot(left, right.T, precision=PRECISE)
    total_rows = lax.axis_size("dp") * left.shape[0]
    total_cols = lax.axis_size("tensor") * right_factor.shape[0]
    factor_scale = 0.5 * math.sqrt(total_rows * total_cols / left.shape[1])
    new_weight = weight - factor_scale * jnp.dot(left, new_factor.T, precision=PRECISE)
    return (new_weight, new_momentum, new_factor)


def solution(mesh):
    in_specs = (P("dp", "tensor"), P("dp", "tensor"), P("dp", "tensor"), P("tensor", None))
    out_specs = (P("dp", "tensor"), P("dp", "tensor"), P("tensor", None))
    return jax.shard_map(
        per_device, mesh=mesh, in_specs=in_specs, out_specs=out_specs, check_vma=False
    )
```

profile of v0, /device:TPU:1, one launch (start us, length us, event | category | flops | bytes accessed | tf_op | source)
XLA Modules:
  0.0 840.5 jit_solution(13724279231924931497)
XLA Ops:
  7.2 0.0 copy-start
  7.2 0.0 copy-start.4
  7.2 0.0 copy-start.3
  7.2 0.0 all-reduce.3.cloned.1.call-start
  7.2 1.6 copy-done
  8.8 2.3 fusion.3
  11.1 12.7 %psum.28 = f32[16,128]{1,0:T(8,128)S(1)} all-reduce(f32[16,128]{1,0:T(8,128)S(1)} %fusion.3), channel_id=1, replica_groups=mesh['dp'=384,'tensor'=2] {'tensor'}, use_global_device_ids=true, to_apply=%region_0.0 | all-reduce | flops 2048 | bytes 16384 | tf_op jit(solution)/shard_map/psum | solution.py:19
  23.8 0.9 fusion.8
  24.7 0.0 all-reduce.3.cloned.1.call-update
  24.8 0.0 all-reduce.5.cloned.1.call-start
  24.8 365.3 %all-reduce.3.cloned.1.call-done = f32[128,128]{0,1:T(8,128)} async-done(((f32[128,128]{0,1:T(8,128)}), f32[128,128]{0,1:T(8,128)}) %all-reduce.3.cloned.1.call-update) | async-done | bytes 65552 | tf_op jit(solution)/shard_map/psum | solution.py:21
  390.1 0.9 copy.8
  391.1 0.9 fusion.7
  391.9 11.7 %cholesky.16 = f32[128,128]{1,0:T(8,128)S(1)} custom-call(f32[128,128]{1,0:T(8,128)S(1)} %fusion.7), custom_call_target="Cholesky" | custom-call | tf_op jit(solution)/shard_map/jit(cholesky)/cholesky | solution.py:22
  403.7 0.6 compare_reduce_fusion
  404.3 0.7 fusion.4
  405.0 9.8 %custom-call.6 = f32[1,128,128]{1,2,0:T(8,128)S(1)} custom-call(f32[1,128,128]{2,1,0:T(8,128)S(1)} %fusion.4), custom_call_target="InvertDiagBlocksLowerTriangular" | custom-call | tf_op jit(solution)/shard_map/triangular_solve | solution.py:12
  414.8 0.2 fusion.5
  414.9 0.0 copy-done.4
  415.0 0.0 copy-done.3
  415.0 5.3 fusion.2
  420.2 0.0 all-reduce.5.cloned.1.call-update
  420.3 394.3 %all-reduce.5.cloned.1.call-done = f32[4608,128]{1,0:T(8,128)} async-done(((f32[4608,128]{1,0:T(8,128)}), f32[4608,128]{1,0:T(8,128)}) %all-reduce.5.cloned.1.call-update) | async-done | bytes 2359312 | tf_op jit(solution)/shard_map/psum | solution.py:24
  814.6 2.3 multiply_reduce_fusion
  816.8 9.4 %psum.31 = f32[128]{0:T(128)S(1)} all-reduce(f32[128]{0:T(128)S(1)} %multiply_reduce_fusion), channel_id=1, replica_groups=mesh['dp'=384,'tensor'=2] {'tensor'}, use_global_device_ids=true, to_apply=%region_6.7 | all-reduce | flops 128 | bytes 1024 | tf_op jit(solution)/shard_map/psum | solution.py:25
  826.2 1.9 broadcast_multiply_fusion
  828.1 0.0 copy-done.5
  828.1 0.0 copy-start.2
  828.1 0.0 copy-start.1
  828.1 2.8 fusion.1
  830.9 0.0 copy-done.1
  830.9 2.8 fusion
  (4 shorter events, 0.0 us)
Async XLA Ops:
  7.2 1.7 copy-start
  7.2 407.8 %copy-start.4 = (bf16[16,4608]{1,0:T(8,128)(2,1)S(1)}, bf16[16,4608]{1,0:T(8,128)(2,1)}, u32[]{:S(2)}) copy-start(bf16[16,4608]{1,0:T(8,128)(2,1)} %param.6) | copy-start | bytes 442372
  7.2 407.8 %copy-start.3 = (f32[16,4608]{1,0:T(8,128)S(1)}, f32[16,4608]{1,0:T(8,128)}, u32[]{:S(2)}) copy-start(f32[16,4608]{1,0:T(8,128)} %param.5) | copy-start | bytes 884740
  7.2 382.9 %all-reduce.3.cloned.1.call-start = ((), (), s32[]{:S(2)}) async-start(), calls=%async_computation | async-start | bytes 131072 | tf_op jit(solution)/shard_map/psum | solution.py:21
  24.8 789.8 %all-reduce.5.cloned.1.call-start = ((), (), s32[]{:S(2)}) async-start(), calls=%async_computation.1 | async-start | bytes 4718592 | tf_op jit(solution)/shard_map/psum | solution.py:24
  826.2 1.9 copy-start.5
  828.1 5.6 copy-start.2
  828.1 2.8 copy-start.1
Sparse Core Ops, SparseCore 0:
  24.9 365.2 all-reduce.2
  420.4 394.1 all-reduce.4
where the time goes:
time: 841 us
  waiting for transfers between devices  760 us (90%)
  other arithmetic  27.9 us (3%)
  blocking collectives  22 us (3%)
  matrix products  14.1 us (2%)
  between operations  14.1 us (2%)
    psum x1, waiting for transfers between devices, per_device(): right = lax.psum(jnp.dot(buffer.T, left, precision=PRECISE), 'dp')  394 us
    psum x1, waiting for transfers between devices, per_device(): gram = lax.psum(gram_part, 'dp')  365 us
  transfers between devices with their start and end apart: 2, of which 2 were waited for; matrix products, arithmetic and copies ran while one was open for 0% of the time, Pallas kernels for 0%

commit v1 on v0

v1 whole, which is shorter than its diff:
```python
import math

import jax
import jax.numpy as jnp
from jax import lax
from jax.sharding import Mesh
from jax.sharding import PartitionSpec as P

PRECISE = lax.Precision.HIGHEST
X, Y, Z = 4, 8, 12
RANK = 128


def gather(block, axis, size):
    return lax.all_to_all(
        jnp.broadcast_to(block[None], (size,) + block.shape), axis, 0, 0, tiled=True
    )


def per_device(weight, momentum, grad, right_factor):
    rows, cols = momentum.shape
    chunk = cols // Z
    piece = 2 * chunk // (X * Y)
    share = 2 * RANK // (2 * Y)
    y_at, z_at = lax.axis_index("y"), lax.axis_index("z")

    buffer = momentum + grad.astype(jnp.float32)
    left_raw = lax.psum(jnp.dot(buffer, right_factor, precision=PRECISE), "core")

    by_z = buffer.reshape(rows, Z, chunk).transpose(1, 0, 2)
    sent = jnp.concatenate([by_z, jnp.broadcast_to(left_raw[None], (Z, rows, RANK))], axis=2)
    held = lax.all_to_all(sent, "z", 0, 0, tiled=True).reshape(Z * rows, chunk + RANK)
    part = lax.dot_general(
        held, held[:, chunk:], (((0,), (0,)), ((), ())), precision=PRECISE
    )

    right_part = part[:chunk].reshape(X, Y // 2, 1, piece, RANK)
    right_part = jnp.broadcast_to(right_part, (X, Y // 2, 2, piece, RANK)).reshape(X * Y, piece, RANK)
    gram_part = lax.dynamic_slice_in_dim(part, chunk + (z_at % Y) * share, share, axis=0)
    gram_part = jnp.broadcast_to(gram_part[None], (X * Y, share, RANK))
    sent = jnp.concatenate([right_part, gram_part], axis=1)
    summed = jnp.sum(lax.all_to_all(sent, ("x", "y"), 0, 0, tiled=True), axis=0)

    by_z = gather(summed, "z", Z)
    gram = by_z[:Y, piece:].reshape(RANK, RANK)
    half = lax.dynamic_slice_in_dim(by_z, (y_at % 2) * (Z // 2), Z // 2, axis=0)[:, :piece]
    by_y = gather(half.reshape(-1, RANK), "y", Y).reshape(-1, RANK)
    by_x = gather(by_y, "x", X)
    right_raw = by_x.reshape(X * Y // 2, Z, piece, RANK).transpose(1, 0, 2, 3).reshape(cols, RANK)

    lower_factor = jnp.linalg.cholesky(gram)
    inverse = lax.linalg.triangular_solve(
        lower_factor, jnp.eye(RANK, dtype=jnp.float32), left_side=True, lower=True
    )
    left = jnp.dot(left_raw, inverse.T, precision=PRECISE)
    right = jnp.dot(right_raw, inverse.T, precision=PRECISE)
    squares = lax.psum(jnp.sum(right * right, axis=0), "core")
    scale = lax.rsqrt(squares + 1e-06)
    new_factor = right * scale
    new_momentum = buffer - (1.0 - 0.95) * jnp.dot(left, right.T, precision=PRECISE)
    factor_scale = 0.5 * math.sqrt(X * Y * Z * rows * 2 * cols / RANK)
    new_weight = weight - factor_scale * jnp.dot(left * scale, right.T, precision=PRECISE)
    return (new_weight, new_momentum, new_factor)


def solution(mesh):
    grid = Mesh(mesh.devices.reshape(X, Y, Z, 2), ("x", "y", "z", "core"))
    dp = ("x", "y", "z")
    in_specs = (P(dp, "core"), P(dp, "core"), P(dp, "core"), P("core", None))
    out_specs = (P(dp, "core"), P(dp, "core"), P("core", None))
    return jax.shard_map(
        per_device, mesh=grid, in_specs=in_specs, out_specs=out_specs, check_vma=False
    )
```

time: 841 us -> 164 us (0.20)
  waiting for transfers between devices: 760 us -> 31.8 us
  blocking collectives: 22 us -> 66.3 us
  starting transfers between devices: 0.08 us -> 17.9 us
  between operations: 14.1 us -> 0.83 us
    psum x2 -> x0, waiting for transfers between devices: 760 us -> none  [the longest x1 394 us: per_device(): right = lax.psum(jnp.dot(buffer.T, left, precision=PRECISE), 'dp')]
    all_to_all x0 -> x2, blocking collectives: none -> 46 us  [the longest x1 24.1 us: per_device(): summed = jnp.sum(lax.all_to_all(sent, ('x', 'y'), 0, 0, tiled=True), axis=0)]
    all_to_all x0 -> x3, waiting for transfers between devices: none -> 31.8 us  [the longest x1 18.2 us: per_device(): lax.all_to_all(sent, 'z', 0, 0, tiled=True).reshape(Z * rows, chunk + RANK)]
    all_to_all x0 -> x3, starting transfers between devices: none -> 17.9 us  [the longest x2 12 us: gather(): lax.all_to_all(jnp.broadcast_to(block[None], (size,) + block.shape), axis...]
  transfers between devices with their start and end apart: 2 -> 3, of which waited for: 2 -> 3; matrix products, arithmetic and copies ran while one was open for 0% -> 14% of each run, Pallas kernels for 0% -> 0%
where the time goes in v1:
time: 164 us; the launch traced here: 162 us
  blocking collectives  66.3 us (40%)
  waiting for transfers between devices  31.8 us (19%)
  other arithmetic  25.7 us (16%)
  starting transfers between devices  17.9 us (11%)
  matrix products  13.5 us (8%)
  local copies, waits for them, and re-layouts  5.99 us (4%)
    all_to_all x1, blocking collectives, per_device(): summed = jnp.sum(lax.all_to_all(sent, ('x', 'y'), 0, 0, tiled=True), axis=0)  24.1 us
    all_to_all x1, blocking collectives, gather(): lax.all_to_all(jnp.broadcast_to(block[None], (size,) + block.shape), axis...  21.9 us
    all_to_all x1, waiting for transfers between devices, per_device(): lax.all_to_all(sent, 'z', 0, 0, tiled=True).reshape(Z * rows, chunk + RANK)  18.2 us
    all_to_all x2, waiting for transfers between devices, gather(): lax.all_to_all(jnp.broadcast_to(block[None], (size,) + block.shape), axis...  13.6 us
    psum x1, blocking collectives, per_device(): lax.psum(jnp.dot(buffer, right_factor, precision=PRECISE), 'core')  12.7 us
    another operation x3, other arithmetic, per_device(): lower_factor = jnp.linalg.cholesky(gram)  12.4 us
    all_to_all x2, starting transfers between devices, gather(): lax.all_to_all(jnp.broadcast_to(block[None], (size,) + block.shape), axis...  12 us
    another operation x2, other arithmetic, per_device(): lax.linalg.triangular_solve(lower_factor, jnp.eye(RANK, dtype=jnp.float32...  10.5 us
  transfers between devices with their start and end apart: 3, of which 3 were waited for; matrix products, arithmetic and copies ran while one was open for 14% of the time, Pallas kernels for 0%

profile of v1, /device:TPU:1, one launch (start us, length us, event | category | flops | bytes accessed | tf_op | source)
XLA Modules:
  0.0 162.1 jit_solution(13927126591458618280)
XLA Ops:
  0.6 0.0 copy-start
  0.6 1.2 convert_add_fusion
  1.8 0.1 reshape.41
  1.9 0.6 copy-done
  2.5 1.3 fusion.10
  3.7 12.7 %psum.14 = f32[16,128]{1,0:T(8,128)S(1)} all-reduce(f32[16,128]{1,0:T(8,128)S(1)} %fusion.10), channel_id=1, replica_groups=mesh['x'=4,'y'=8,'z'=12,'core'=2] {'core'}, use_global_device_ids=true, to_apply=%region_0.0 | all-reduce | flops 2048 | bytes 16384 | tf_op jit(solution)/shard_map/psum | solution.py:28
  16.5 1.0 copy.17
  17.5 5.9 %all-to-all-start = ((f32[12,16,512]{2,1,0:T(8,128)}), f32[12,16,512]{2,1,0:T(8,128)S(1)}, u32[]{:S(2)}, u32[]{:S(2)}) async-start(f32[12,16,512]{2,1,0:T(8,128)} %copy.17), calls=%async_computation | async-start | bytes 786432 | tf_op jit(solution)/shard_map/all_to_all | solution.py:32
  23.4 18.2 %all-to-all-done = f32[12,16,512]{2,1,0:T(8,128)S(1)} async-done(((f32[12,16,512]{2,1,0:T(8,128)}), f32[12,16,512]{2,1,0:T(8,128)S(1)}, u32[]{:S(2)}, u32[]{:S(2)}) %all-to-all-start) | async-done | bytes 393248 | tf_op jit(solution)/shard_map/all_to_all | solution.py:32
  41.6 1.1 fusion.2
  42.8 24.1 %all_to_all.25 = f32[32,40,128]{2,1,0:T(8,128)S(1)} all-to-all(f32[32,40,128]{2,1,0:T(8,128)S(1)} %pad_maximum_fusion), channel_id=1, replica_groups=mesh['x'=4,'y'=8,'z'=12,'core'=2] {'x','y'}, dimensions={0} | all-to-all | bytes 1310720 | tf_op jit(solution)/shard_map/all_to_all | solution.py:42
  66.9 0.1 reduce_sum.18
  66.9 0.7 broadcast_in_dim.24
  67.7 6.7 %all-to-all-start.2 = ((f32[12,40,128]{2,1,0:T(8,128)}), f32[12,40,128]{2,1,0:T(8,128)S(1)}, u32[]{:S(2)}, u32[]{:S(2)}) async-start(f32[12,40,128]{2,1,0:T(8,128)} %broadcast_in_dim.24), calls=%async_computation.2 | async-start | bytes 491520 | tf_op jit(solution)/shard_map/all_to_all | solution.py:15
  74.4 11.7 %all-to-all-done.2 = f32[12,40,128]{2,1,0:T(8,128)S(1)} async-done(((f32[12,40,128]{2,1,0:T(8,128)}), f32[12,40,128]{2,1,0:T(8,128)S(1)}, u32[]{:S(2)}, u32[]{:S(2)}) %all-to-all-start.2) | async-done | bytes 245792 | tf_op jit(solution)/shard_map/all_to_all | solution.py:15
  86.1 21.9 %all_to_all.26 = f32[8,144,128]{2,1,0:T(8,128)S(1)} all-to-all(f32[8,144,128]{2,1,0:T(8,128)S(1)} %broadcast_in_dim.49), channel_id=1, replica_groups=mesh['x'=4,'y'=8,'z'=12,'core'=2] {'y'}, dimensions={0} | all-to-all | bytes 1179648 | tf_op jit(solution)/shard_map/all_to_all | solution.py:15
  108.0 1.6 broadcast_in_dim.51
  109.6 5.3 %all-to-all-start.4 = ((f32[4,1152,128]{2,1,0:T(8,128)}), f32[4,1152,128]{2,1,0:T(8,128)}, u32[]{:S(2)}, u32[]{:S(2)}) async-start(f32[4,1152,128]{2,1,0:T(8,128)} %broadcast_in_dim.51), calls=%async_computation.4 | async-start | bytes 4718592 | tf_op jit(solution)/shard_map/all_to_all | solution.py:15
  114.9 0.1 copy.18
  115.0 11.7 %cholesky.17 = f32[128,128]{1,0:T(8,128)S(1)} custom-call(f32[128,128]{1,0:T(8,128)S(1)} %fusion.7), custom_call_target="Cholesky" | custom-call | tf_op jit(solution)/shard_map/jit(cholesky)/cholesky | solution.py:51
  126.8 0.6 compare_reduce_fusion
  127.4 0.7 fusion.4
  128.1 9.8 %custom-call.6 = f32[1,128,128]{1,2,0:T(8,128)S(1)} custom-call(f32[1,128,128]{2,1,0:T(8,128)S(1)} %fusion.4), custom_call_target="InvertDiagBlocksLowerTriangular" | custom-call | tf_op jit(solution)/shard_map/triangular_solve | solution.py:52
  137.9 0.2 fusion.5
  138.1 0.2 fusion.11
  138.3 1.9 %all-to-all-done.4 = f32[4,1152,128]{2,1,0:T(8,128)} async-done(((f32[4,1152,128]{2,1,0:T(8,128)}), f32[4,1152,128]{2,1,0:T(8,128)}, u32[]{:S(2)}, u32[]{:S(2)}) %all-to-all-start.4) | async-done | bytes 2359328 | tf_op jit(solution)/shard_map/all_to_all | solution.py:15
  140.2 1.9 %copy.19 = f32[12,16,24,128]{3,2,1,0:T(8,128)S(1)} copy(f32[12,16,24,128]{3,2,0,1:T(8,128)} %bitcast.11) | data formatting | bytes 4718592 | tf_op jit(solution)/shard_map/transpose | solution.py:49
  142.1 3.4 %multiply_reduce_fusion = (f32[128]{0:T(128)S(1)}, f32[4608,128]{1,0:T(8,128)}) fusion(f32[4608,128]{1,0:T(8,128)S(1)} %bitcast.31, f32[128,128]{1,0:T(8,128)S(1)} %fusion.5), kind=kOutput, calls=%fused_computation.4 | convolution fusion | flops 907149184 | bytes 4784640 | tf_op jit(solution)/shard_map/dot_general | solution.py:56
  145.5 7.6 %psum.15 = f32[128]{0:T(128)S(1)} all-reduce(f32[128]{0:T(128)S(1)} %get-tuple-element.3), channel_id=1, replica_groups=mesh['x'=4,'y'=8,'z'=12,'core'=2] {'core'}, use_global_device_ids=true, to_apply=%region_5.6 | all-reduce | flops 128 | bytes 1024 | tf_op jit(solution)/shard_map/psum | solution.py:57
  153.2 4.6 %fusion = f32[16,4608]{1,0:T(8,128)} fusion(f32[16,4608]{1,0:T(8,128)S(1)} %convert_add_fusion, f32[16,128]{1,0:T(8,128)S(1)} %fusion.11, f32[4608,128]{1,0:T(8,128)} %get-tuple-element.4), kind=kOutput, calls=%fused_computation.1 | convolution fusion | flops 113393664 | bytes 2957312 | tf_op jit(solution)/shard_map/dot_general | solution.py:60
  157.7 1.6 broadcast_multiply_fusion
  159.3 2.8 %fusion.1 = f32[16,4608]{1,0:T(8,128)} fusion(f32[16,4608]{1,0:T(8,128)S(1)} %copy-done.2, f32[4608,128]{1,0:T(8,128)S(1)} %copy-done.1, f32[16,128]{1,0:T(8,128)S(1)} %fusion.11, f32[128]{0:T(128)S(1)} %add_rsqrt_fusion), kind=kOutput, calls=%fused_computation.3 | convolution fusion | flops 113395712 | bytes 2957824 | tf_op jit(solution)/shard_map/dot_general | solution.py:62
  (17 shorter events, 0.3 us)
Async XLA Ops:
  0.6 1.8 %copy-start = (f32[4608,128]{1,0:T(8,128)S(1)}, f32[4608,128]{1,0:T(8,128)}, u32[]{:S(2)}) copy-start(f32[4608,128]{1,0:T(8,128)} %param.7) | copy-start | bytes 7077892
  17.5 24.1 %all-to-all-start = ((f32[12,16,512]{2,1,0:T(8,128)}), f32[12,16,512]{2,1,0:T(8,128)S(1)}, u32[]{:S(2)}, u32[]{:S(2)}) async-start(f32[12,16,512]{2,1,0:T(8,128)} %copy.17), calls=%async_computation | async-start | bytes 786432 | tf_op jit(solution)/shard_map/all_to_all | solution.py:32
  67.7 18.4 %all-to-all-start.2 = ((f32[12,40,128]{2,1,0:T(8,128)}), f32[12,40,128]{2,1,0:T(8,128)S(1)}, u32[]{:S(2)}, u32[]{:S(2)}) async-start(f32[12,40,128]{2,1,0:T(8,128)} %broadcast_in_dim.24), calls=%async_computation.2 | async-start | bytes 491520 | tf_op jit(solution)/shard_map/all_to_all | solution.py:15
  109.6 30.7 %all-to-all-start.4 = ((f32[4,1152,128]{2,1,0:T(8,128)}), f32[4,1152,128]{2,1,0:T(8,128)}, u32[]{:S(2)}, u32[]{:S(2)}) async-start(f32[4,1152,128]{2,1,0:T(8,128)} %broadcast_in_dim.51), calls=%async_computation.4 | async-start | bytes 4718592 | tf_op jit(solution)/shard_map/all_to_all | solution.py:15
  153.2 4.6 %copy-start.1 = (f32[4608,128]{1,0:T(8,128)S(1)}, f32[4608,128]{1,0:T(8,128)}, u32[]{:S(2)}) copy-start(f32[4608,128]{1,0:T(8,128)} %get-tuple-element.4) | copy-start | bytes 7077892
  157.7 1.6 copy-start.2

commit v2 on v1

v2 whole, which is shorter than its diff:
```python
import functools
import math

import jax
import jax.numpy as jnp
from jax import lax
from jax.experimental import pallas as pl
from jax.experimental.pallas import tpu as pltpu
from jax.sharding import Mesh
from jax.sharding import PartitionSpec as P

PRECISE = lax.Precision.HIGHEST
X, Y, Z = 4, 8, 12
RANK = 128
NT = (((1,), (1,)), ((), ()))
TN = (((0,), (0,)), ((), ()))
VM = pl.BlockSpec(memory_space=pltpu.VMEM)
SM = pl.BlockSpec(memory_space=pltpu.SMEM)


def params():
    return pltpu.CompilerParams(vmem_limit_bytes=32 * 1024 * 1024)


def factor_kernel(gram_ref, inverse_ref, work):
    step = 8
    row = lax.broadcasted_iota(jnp.int32, (RANK, RANK), 0)
    col = lax.broadcasted_iota(jnp.int32, (RANK, RANK), 1)
    work[:, :RANK] = gram_ref[...]
    work[:, RANK:] = (row == col).astype(jnp.float32)
    for at in range(0, RANK, step):
        block = work[at : at + step, :]
        rows = [block[i : i + 1, :] for i in range(step)]
        corner = block[:, at : at + step]
        entry = {
            (i, j): jnp.broadcast_to(corner[i : i + 1, j : j + 1], (1, RANK))
            for i in range(step) for j in range(i, step)
        }
        for i in range(step):
            scale = lax.rsqrt(entry[i, i])
            pivot = {j: entry[i, j] * scale for j in range(i + 1, step)}
            rows[i] = rows[i] * jnp.concatenate([scale, scale], axis=1)
            for j in range(i + 1, step):
                wide = jnp.concatenate([pivot[j], pivot[j]], axis=1)
                rows[j] = rows[j] - wide * rows[i]
                for k in range(j, step):
                    entry[j, k] = entry[j, k] - pivot[j] * pivot[k]
        done = jnp.concatenate(rows, axis=0)
        inverse_ref[at : at + step, :] = done[:, RANK:]
        if at + step < RANK:
            change = lax.dot_general(done[:, :RANK], done, TN, precision=PRECISE, preferred_element_type=jnp.float32)
            work[at + step :, :] = work[at + step :, :] - change[at + step :, :]

def factor(gram):
    return pl.pallas_call(factor_kernel, out_shape=jax.ShapeDtypeStruct((RANK,RANK),jnp.float32),
        in_specs=[VM], out_specs=VM, scratch_shapes=[pltpu.VMEM((RANK,2*RANK),jnp.float32)],
        compiler_params=params(), name="factor")(gram)

def order_kernel(pieces, shares, by_y_ref, right_ref, gram_ref):
    Y, Z, piece, share = by_y_ref.shape[0], pieces[0], pieces[1], shares
    pitch = piece + share
    for y in range(Y):
        for z in range(Z):
            right_ref[(z*Y+y)*piece:(z*Y+y+1)*piece, :] = by_y_ref[y, z*pitch:z*pitch+piece, :]
        for z in range(4):
            gram_ref[(y*4+z)*share:(y*4+z+1)*share, :] = by_y_ref[y, z*pitch+piece:(z+1)*pitch, :]

def order(by_y):
    return pl.pallas_call(functools.partial(order_kernel,(12,12),4),
        out_shape=(jax.ShapeDtypeStruct((1152,RANK),jnp.float32),jax.ShapeDtypeStruct((RANK,RANK),jnp.float32)),
        in_specs=[VM],out_specs=(VM,VM),compiler_params=params(),name="order")(by_y)

def split(value):
    high = value.astype(jnp.bfloat16)
    return high, (value - high.astype(jnp.float32)).astype(jnp.bfloat16)

def right_kernel(at_ref, b0, b1, b2, b3, inverse_ref, left_raw_ref, right_ref, squares_ref, left_ref):
    X, Z, piece = 4, 12, 96
    inverse = inverse_ref[...]
    left_ref[...] = lax.dot_general(left_raw_ref[...], inverse, NT, precision=PRECISE, preferred_element_type=jnp.float32)
    high, low = split(inverse)
    factors = jnp.concatenate([jnp.concatenate([high, high], axis=1),
        jnp.concatenate([low, jnp.zeros_like(low)], axis=1)], axis=0)
    total = jnp.zeros((8, RANK), jnp.float32)
    for back, block in enumerate((b0, b1, b2, b3)):
        x = lax.rem(at_ref[0] + (X - back), X)
        for z in range(Z):
            both = jnp.concatenate(split(block[z*piece:(z+1)*piece, :]), axis=1)
            out = lax.dot_general(both, factors, NT, preferred_element_type=jnp.float32)
            out = out[:, :RANK] + out[:, RANK:]
            right_ref[pl.ds(pl.multiple_of(z*X*piece + x*piece, 8), piece), :] = out
            total = total + jnp.sum((out*out).reshape(piece//8, 8, RANK), axis=0)
    squares_ref[...] = jnp.sum(total, axis=0, keepdims=True)

def right_of(at, blocks, inverse, left_raw):
    return pl.pallas_call(right_kernel,
        out_shape=(jax.ShapeDtypeStruct((4608,RANK),jnp.float32),jax.ShapeDtypeStruct((1,RANK),jnp.float32),jax.ShapeDtypeStruct((16,RANK),jnp.float32)),
        in_specs=[SM]+[VM]*6,out_specs=(VM,VM,VM),compiler_params=params(),name="right")(at,*blocks,inverse,left_raw)

def update_kernel(decay, gain, right_ref, squares_ref, left_ref, buffer_ref, weight_ref, weight_out, momentum_out, factor_out):
    tile = 512
    scale = lax.rsqrt(squares_ref[...] + 1e-06)
    left = left_ref[...]
    high, low = split(jnp.concatenate([decay*left, (gain*left)*scale], axis=0))
    both_left = jnp.concatenate([jnp.concatenate([high, high], axis=1), jnp.concatenate([low, jnp.zeros_like(low)], axis=1)], axis=0)
    n = left.shape[0]
    for at in range(0, right_ref.shape[0], tile):
        right = right_ref[at:at+tile, :]
        factor_out[at:at+tile, :] = right * scale
        both = jnp.concatenate(split(right), axis=1)
        out = lax.dot_general(both_left, both, NT, preferred_element_type=jnp.float32)
        out = out[:2*n] + out[2*n:]
        momentum_out[:, at:at+tile] = buffer_ref[:, at:at+tile] - out[:n]
        weight_out[:, at:at+tile] = weight_ref[:, at:at+tile] - out[n:]

def update(decay, gain, right, squares, left, buffer, weight):
    return pl.pallas_call(functools.partial(update_kernel,decay,gain),
        out_shape=(jax.ShapeDtypeStruct(weight.shape,jnp.float32),jax.ShapeDtypeStruct(weight.shape,jnp.float32),jax.ShapeDtypeStruct(right.shape,jnp.float32)),
        in_specs=[VM]*5,out_specs=(VM,VM,VM),compiler_params=params(),name="update")(right,squares,left,buffer,weight)


def gather(block, axis, size):
    return lax.all_to_all(
        jnp.broadcast_to(block[None], (size,) + block.shape), axis, 0, 0, tiled=True
    )


def per_device(weight, momentum, grad, right_factor):
    rows, cols = momentum.shape
    chunk = cols // Z
    piece = chunk // (X * Y)
    share = RANK // (4 * Y)
    x_at, z_at = lax.axis_index("x"), lax.axis_index("z")

    buffer = momentum + grad.astype(jnp.float32)
    left_raw = lax.psum(jnp.dot(buffer, right_factor, precision=PRECISE), "core")

    by_z = buffer.reshape(rows, Z, chunk).transpose(1, 0, 2)
    sent = jnp.concatenate([by_z, jnp.broadcast_to(left_raw[None], (Z, rows, RANK))], axis=2)
    held = lax.all_to_all(sent, "z", 0, 0, tiled=True).reshape(Z * rows, chunk + RANK)
    part = lax.dot_general(held, held[:, chunk:], TN, precision=PRECISE)

    right_part = part[:chunk].reshape(X * Y, piece, RANK)
    gram_part = part[chunk:].reshape(Y, 4, share, RANK)
    gram_part = lax.dynamic_index_in_dim(gram_part, z_at % 4, axis=1, keepdims=False)
    gram_part = jnp.broadcast_to(gram_part[None], (X, Y, share, RANK)).reshape(X * Y, share, RANK)
    sent = jnp.concatenate([right_part, gram_part], axis=1)
    summed = jnp.sum(lax.all_to_all(sent, ("x", "y"), 0, 0, tiled=True), axis=0)

    by_z = gather(summed, "z", Z).reshape(-1, RANK)
    by_y = gather(by_z, "y", Y)
    own, gram = order(by_y)
    blocks = [own] + [
        lax.ppermute(own, "x", [(i, (i + k) % X) for i in range(X)]) for k in range(1, X)
    ]
    inverse = factor(gram)
    right, squares, left = right_of(x_at.reshape(1), blocks, inverse, left_raw)
    squares = lax.psum(squares, "core")
    gain = 0.5 * math.sqrt(X * Y * Z * rows * 2 * cols / RANK)
    return update(1.0 - 0.95, gain, right, squares, left, buffer, weight)


def solution(mesh):
    grid = Mesh(mesh.devices.reshape(X, Y, Z, 2), ("x", "y", "z", "core"))
    dp = ("x", "y", "z")
    in_specs = (P(dp, "core"), P(dp, "core"), P(dp, "core"), P("core", None))
    out_specs = (P(dp, "core"), P(dp, "core"), P("core", None))
    return jax.shard_map(
        per_device, mesh=grid, in_specs=in_specs, out_specs=out_specs, check_vma=False
    )
```

time: 164 us -> 148 us (0.902)
  other arithmetic: 25.7 us -> 1.29 us
  Pallas kernels: 0 us -> 13.9 us
  matrix products: 13.5 us -> 2.35 us
  blocking collectives: 66.3 us -> 74 us
  starting transfers between devices: 17.9 us -> 14.1 us
  waiting for transfers between devices: 31.8 us -> 34 us
    another operation x5 -> x0, other arithmetic: 22.9 us -> none  [the longest x3 12.4 us: per_device(): lower_factor = jnp.linalg.cholesky(gram)]
    all_to_all x1 -> x2, blocking collectives: 21.9 us -> 37.9 us  [gather(): lax.all_to_all(jnp.broadcast_to(block[None], (size,) + block.shape), axis...]
    ppermute x0 -> x3, waiting for transfers between devices: none -> 15.8 us  [per_device(): lax.ppermute(own, 'x', [(i, (i + k) % X) for i in range(X)])]
    pallas_call x0 -> x4, Pallas kernels: none -> 13.9 us  [the longest x1 7.84 us: factor(): pl.pallas_call(factor_kernel, out_shape=jax.ShapeDtypeStruct((RANK, RANK)...]
    all_to_all x2 -> x0, waiting for transfers between devices: 13.6 us -> none  [gather(): lax.all_to_all(jnp.broadcast_to(block[None], (size,) + block.shape), axis...]
    all_to_all x2 -> x0, starting transfers between devices: 12 us -> none  [gather(): lax.all_to_all(jnp.broadcast_to(block[None], (size,) + block.shape), axis...]
    dot_general x5 -> x1, matrix products: 12 us -> 1.08 us  [per_device(): part = lax.dot_general(held, held[:, chunk:], TN, precision=PRECISE)]
    ppermute x0 -> x3, starting transfers between devices: none -> 8.27 us  [per_device(): lax.ppermute(own, 'x', [(i, (i + k) % X) for i in range(X)])]
  transfers between devices with their start and end apart: 3 -> 4, of which waited for: 3 -> 2; matrix products, arithmetic and copies ran while one was open for 14% -> 0% of each run, Pallas kernels for 0% -> 5%
where the time goes in v2:
time: 148 us; the launch traced here: 147 us
  blocking collectives  74 us (50%)
  waiting for transfers between devices  34 us (23%)
  starting transfers between devices  14.1 us (10%)
  Pallas kernels  13.9 us (9%)
  local copies, waits for them, and re-layouts  6.79 us (5%)
  matrix products  2.35 us (2%)
    all_to_all x2, blocking collectives, gather(): lax.all_to_all(jnp.broadcast_to(block[None], (size,) + block.shape), axis...  37.9 us
    all_to_all x1, blocking collectives, per_device(): summed = jnp.sum(lax.all_to_all(sent, ('x', 'y'), 0, 0, tiled=True), axis=0)  19.1 us
    all_to_all x1, waiting for transfers between devices, per_device(): lax.all_to_all(sent, 'z', 0, 0, tiled=True).reshape(Z * rows, chunk + RANK)  18.2 us
    ppermute x3, waiting for transfers between devices, per_device(): lax.ppermute(own, 'x', [(i, (i + k) % X) for i in range(X)])  15.8 us
    psum x1, blocking collectives, per_device(): lax.psum(jnp.dot(buffer, right_factor, precision=PRECISE), 'core')  12.7 us
    ppermute x3, starting transfers between devices, per_device(): lax.ppermute(own, 'x', [(i, (i + k) % X) for i in range(X)])  8.27 us
    pallas_call x1, Pallas kernels, factor(): pl.pallas_call(factor_kernel, out_shape=jax.ShapeDtypeStruct((RANK, RANK)...  7.84 us
    all_to_all x1, starting transfers between devices, per_device(): lax.all_to_all(sent, 'z', 0, 0, tiled=True).reshape(Z * rows, chunk + RANK)  5.86 us
  transfers between devices with their start and end apart: 4, of which 2 were waited for; matrix products, arithmetic and copies ran while one was open for 0% of the time, Pallas kernels for 5%

profile of v2, /device:TPU:1, one launch (start us, length us, event | category | flops | bytes accessed | tf_op | source)
XLA Modules:
  0.0 147.3 jit_solution(9596313764485552641)
XLA Ops:
  0.6 0.0 copy-start
  0.6 1.2 convert_add_fusion.buffer_ref
  1.8 0.1 reshape.30
  1.9 0.6 copy-done
  2.5 1.3 fusion.2
  3.7 12.7 %psum.14.left_raw_ref = f32[16,128]{1,0:T(8,128)S(1)} all-reduce(f32[16,128]{1,0:T(8,128)S(1)} %fusion.2), channel_id=1, replica_groups=mesh['x'=4,'y'=8,'z'=12,'core'=2] {'core'}, use_global_device_ids=true, to_apply=%region_0.0 | all-reduce | flops 2048 | bytes 16384 | tf_op jit(solution)/shard_map/psum | solution.py:136
  16.5 1.0 copy.8
  17.5 5.9 %all-to-all-start = ((f32[12,16,512]{2,1,0:T(8,128)}), f32[12,16,512]{2,1,0:T(8,128)S(1)}, u32[]{:S(2)}, u32[]{:S(2)}) async-start(f32[12,16,512]{2,1,0:T(8,128)} %copy.8), calls=%async_computation | async-start | bytes 786432 | tf_op jit(solution)/shard_map/all_to_all | solution.py:140
  23.4 18.2 %all-to-all-done = f32[12,16,512]{2,1,0:T(8,128)S(1)} async-done(((f32[12,16,512]{2,1,0:T(8,128)}), f32[12,16,512]{2,1,0:T(8,128)S(1)}, u32[]{:S(2)}, u32[]{:S(2)}) %all-to-all-start) | async-done | bytes 393248 | tf_op jit(solution)/shard_map/all_to_all | solution.py:140
  41.6 1.1 fusion
  42.8 19.1 %all_to_all.20 = f32[32,16,128]{2,1,0:T(8,128)S(1)} all-to-all(f32[32,16,128]{2,1,0:T(8,128)S(1)} %pad_maximum_fusion.1), channel_id=1, replica_groups=mesh['x'=4,'y'=8,'z'=12,'core'=2] {'x','y'}, dimensions={0} | all-to-all | bytes 524288 | tf_op jit(solution)/shard_map/all_to_all | solution.py:148
  62.0 14.9 %all_to_all.21 = f32[12,16,128]{2,1,0:T(8,128)S(1)} all-to-all(f32[12,16,128]{2,1,0:T(8,128)S(1)} %broadcast_in_dim.30), channel_id=1, replica_groups=mesh['x'=4,'y'=8,'z'=12,'core'=2] {'z'}, dimensions={0} | all-to-all | bytes 196608 | tf_op jit(solution)/shard_map/all_to_all | solution.py:123
  76.8 0.1 broadcast_in_dim.32
  76.9 0.0 copy-start.3
  76.9 23.1 %all_to_all.22.by_y_ref = f32[8,192,128]{2,1,0:T(8,128)S(1)} all-to-all(f32[8,192,128]{2,1,0:T(8,128)S(1)} %broadcast_in_dim.32), channel_id=1, replica_groups=mesh['x'=4,'y'=8,'z'=12,'core'=2] {'y'}, dimensions={0} | all-to-all | bytes 1572864 | tf_op jit(solution)/shard_map/all_to_all | solution.py:123
  100.0 0.1 order.1
  100.0 0.0 copy-start.4
  100.1 0.6 copy-done.4
  100.7 2.8 %collective-permute-start.2 = (f32[1152,128]{1,0:T(8,128)S(1)}, f32[1152,128]{1,0:T(8,128)}, u32[]{:S(2)}, u32[]{:S(2)}) collective-permute-start(f32[1152,128]{1,0:T(8,128)S(1)} %get-tuple-element.8.b0), channel_id=1, source_target_pairs={{0,576},{192,0},{384,192},{576,384},{1,577},{193,1},{385,193},{577... | collective-permute-start | bytes 1769480 | tf_op jit(solution)/shard_map/ppermute | solution.py:154
  103.5 3.1 %collective-permute-start.1 = (f32[1152,128]{1,0:T(8,128)S(1)}, f32[1152,128]{1,0:T(8,128)}, u32[]{:S(2)}, u32[]{:S(2)}) collective-permute-start(f32[1152,128]{1,0:T(8,128)S(1)} %get-tuple-element.8.b0), channel_id=1, source_target_pairs={{0,384},{192,576},{384,0},{576,192},{1,385},{193,577},{385,1},{577... | collective-permute-start | bytes 1769480 | tf_op jit(solution)/shard_map/ppermute | solution.py:154
  106.6 2.3 %collective-permute-start = (f32[1152,128]{1,0:T(8,128)S(1)}, f32[1152,128]{1,0:T(8,128)}, u32[]{:S(2)}, u32[]{:S(2)}) collective-permute-start(f32[1152,128]{1,0:T(8,128)S(1)} %get-tuple-element.8.b0), channel_id=1, source_target_pairs={{0,192},{192,384},{384,576},{576,0},{1,193},{193,385},{385,577},{5... | collective-permute-start | bytes 1769480 | tf_op jit(solution)/shard_map/ppermute | solution.py:154
  109.0 0.0 copy-start.5
  109.0 0.8 copy-done.5
  109.8 7.8 %factor.1.inverse_ref = f32[128,128]{1,0:T(8,128)S(1)} custom-call(f32[128,128]{1,0:T(8,128)S(1)} %copy-done.5), custom_call_target="tpu_custom_call" | custom-call | tf_op jit(solution)/shard_map/factor/pallas_call | solution.py:55
  117.7 15.7 %collective-permute-done.b1 = f32[1152,128]{1,0:T(8,128)} collective-permute-done((f32[1152,128]{1,0:T(8,128)S(1)}, f32[1152,128]{1,0:T(8,128)}, u32[]{:S(2)}, u32[]{:S(2)}) %collective-permute-start) | collective-permute-done | bytes 589856 | tf_op jit(solution)/shard_map/ppermute | solution.py:154
  133.4 3.5 %right.1 = (f32[4608,128]{1,0:T(8,128)S(1)}, f32[1,128]{1,0:T(1,128)S(1)}, f32[16,128]{1,0:T(8,128)S(1)}) custom-call(s32[1]{0:T(128)} %bitcast.at_ref, f32[1152,128]{1,0:T(8,128)S(1)} %get-tuple-element.8.b0, f32[1152,128]{1,0:T(8,128)} %collective-permute-done.b1, f32[1152,128]{1,0:T(8,128)} %collective-permute-done.1.b2, ...), custom_call_target="tpu_custom_call" | custom-call | tf_op jit(solution)/shard_map/right/pallas_call | solution.py:96
  137.0 0.0 copy-start.1
  137.0 1.4 copy-done.1
  138.4 0.5 copy-done.6
  138.9 4.2 %psum.15.squares_ref = f32[1,128]{1,0:T(1,128)S(1)} all-reduce(f32[1,128]{1,0:T(1,128)} %copy-done.6), channel_id=1, replica_groups=mesh['x'=4,'y'=8,'z'=12,'core'=2] {'core'}, use_global_device_ids=true, to_apply=%region_2.3 | all-reduce | flops 128 | bytes 1024 | tf_op jit(solution)/shard_map/psum | solution.py:158
  143.1 1.7 %copy-done.2 = f32[4608,128]{1,0:T(8,128)S(1)} copy-done((f32[4608,128]{1,0:T(8,128)S(1)}, f32[4608,128]{1,0:T(8,128)}, u32[]{:S(2)}) %copy-start.2) | copy-done | bytes 2359320
  144.8 2.5 %update.1 = (f32[16,4608]{1,0:T(8,128)}, f32[16,4608]{1,0:T(8,128)}, f32[4608,128]{1,0:T(8,128)}) custom-call(f32[4608,128]{1,0:T(8,128)S(1)} %copy-done.2, f32[1,128]{1,0:T(1,128)S(1)} %psum.15.squares_ref, f32[16,128]{1,0:T(8,128)S(1)} %get-tuple-element.12.left_ref, f32[16,4608]{1,0:T(8,128)S(1)} %convert_add_fusion.buffer_ref, f32[16,4608]{1,0:T(8,128)S(1)} %copy-done.3), custom_call_target="tpu_custom_call" | custom-call | tf_op jit(solution)/shard_map/update/pallas_call | solution.py:117
  (15 shorter events, 0.2 us)
Async XLA Ops:
  0.6 1.8 %copy-start = (f32[4608,128]{1,0:T(8,128)S(1)}, f32[4608,128]{1,0:T(8,128)}, u32[]{:S(2)}) copy-start(f32[4608,128]{1,0:T(8,128)} %param.7) | copy-start | bytes 7077892
  17.5 24.1 %all-to-all-start = ((f32[12,16,512]{2,1,0:T(8,128)}), f32[12,16,512]{2,1,0:T(8,128)S(1)}, u32[]{:S(2)}, u32[]{:S(2)}) async-start(f32[12,16,512]{2,1,0:T(8,128)} %copy.8), calls=%async_computation | async-start | bytes 786432 | tf_op jit(solution)/shard_map/all_to_all | solution.py:140
  76.9 66.2 %copy-start.3 = (f32[16,4608]{1,0:T(8,128)S(1)}, f32[16,4608]{1,0:T(8,128)}, u32[]{:S(2)}) copy-start(f32[16,4608]{1,0:T(8,128)} %weight_ref.1) | copy-start | bytes 884740
  100.0 0.6 copy-start.4
  100.7 17.0 %collective-permute-start.2 = (f32[1152,128]{1,0:T(8,128)S(1)}, f32[1152,128]{1,0:T(8,128)}, u32[]{:S(2)}, u32[]{:S(2)}) collective-permute-start(f32[1152,128]{1,0:T(8,128)S(1)} %get-tuple-element.8.b0), channel_id=1, source_target_pairs={{0,576},{192,0},{384,192},{576,384},{1,577},{193,1},{385,193},{577... | collective-permute-start | bytes 1769480 | tf_op jit(solution)/shard_map/ppermute | solution.py:154
  103.5 14.2 %collective-permute-start.1 = (f32[1152,128]{1,0:T(8,128)S(1)}, f32[1152,128]{1,0:T(8,128)}, u32[]{:S(2)}, u32[]{:S(2)}) collective-permute-start(f32[1152,128]{1,0:T(8,128)S(1)} %get-tuple-element.8.b0), channel_id=1, source_target_pairs={{0,384},{192,576},{384,0},{576,192},{1,385},{193,577},{385,1},{577... | collective-permute-start | bytes 1769480 | tf_op jit(solution)/shard_map/ppermute | solution.py:154
  106.6 26.8 %collective-permute-start = (f32[1152,128]{1,0:T(8,128)S(1)}, f32[1152,128]{1,0:T(8,128)}, u32[]{:S(2)}, u32[]{:S(2)}) collective-permute-start(f32[1152,128]{1,0:T(8,128)S(1)} %get-tuple-element.8.b0), channel_id=1, source_target_pairs={{0,192},{192,384},{384,576},{576,0},{1,193},{193,385},{385,577},{5... | collective-permute-start | bytes 1769480 | tf_op jit(solution)/shard_map/ppermute | solution.py:154
  109.0 0.8 copy-start.5
  137.0 1.4 copy-start.1
  138.4 0.5 copy-start.6
  143.1 1.7 %copy-start.2 = (f32[4608,128]{1,0:T(8,128)S(1)}, f32[4608,128]{1,0:T(8,128)}, u32[]{:S(2)}) copy-start(f32[4608,128]{1,0:T(8,128)} %copy-done.1) | copy-start | bytes 7077892

commit v3 on v2

v3 whole, which is shorter than its diff:
```python
import functools
import math

import jax
import jax.numpy as jnp
from jax import lax
from jax.experimental import pallas as pl
from jax.experimental.pallas import tpu as pltpu
from jax.sharding import Mesh
from jax.sharding import PartitionSpec as P

PRECISE = lax.Precision.HIGHEST
X, J, K, B = 4, 4, 6, 2
NEAR, FAR = ("x", "yb", "zb"), ("yj", "zk")
RANK = 128
NT = (((1,), (1,)), ((), ()))
TN = (((0,), (0,)), ((), ()))
VM = pl.BlockSpec(memory_space=pltpu.VMEM)


def params():
    return pltpu.CompilerParams(vmem_limit_bytes=16 * 1024 * 1024)


def factor_kernel(gram_ref, inverse_ref, work):
    step = 8
    row = lax.broadcasted_iota(jnp.int32, (RANK, RANK), 0)
    col = lax.broadcasted_iota(jnp.int32, (RANK, RANK), 1)
    half = RANK // 2
    rest = gram_ref[half:, :]
    nothing = jnp.zeros((half // 2, half), jnp.float32)
    work[:half, :RANK] = gram_ref[:half, :]
    work[half : half + half // 2, :RANK] = jnp.concatenate([nothing, rest[:, :half]], axis=1)
    work[half + half // 2 :, :RANK] = jnp.concatenate([nothing, rest[:, half:]], axis=1)
    work[:, RANK:] = (row == col).astype(jnp.float32)
    for at in range(0, RANK, step):
        block = work[at : at + step, :]
        rows = [block[i : i + 1, :] for i in range(step)]
        corner = block[:, at : at + step]
        entry = {
            (i, j): jnp.broadcast_to(corner[i : i + 1, j : j + 1], (1, RANK))
            for i in range(step) for j in range(i, step)
        }
        for i in range(step):
            scale = lax.rsqrt(entry[i, i])
            pivot = {j: entry[i, j] * scale for j in range(i + 1, step)}
            rows[i] = rows[i] * jnp.concatenate([scale, scale], axis=1)
            for j in range(i + 1, step):
                wide = jnp.concatenate([pivot[j], pivot[j]], axis=1)
                rows[j] = rows[j] - wide * rows[i]
                for k in range(j, step):
                    entry[j, k] = entry[j, k] - pivot[j] * pivot[k]
        done = jnp.concatenate(rows, axis=0)
        inverse_ref[at : at + step, :] = done[:, RANK:]
        if at + step < RANK:
            change = lax.dot_general(done[:, :RANK], done, TN, precision=PRECISE, preferred_element_type=jnp.float32)
            work[at + step :, :] = work[at + step :, :] - change[at + step :, :]

def factor(gram):
    return pl.pallas_call(factor_kernel, out_shape=jax.ShapeDtypeStruct((RANK,RANK),jnp.float32),
        in_specs=[VM], out_specs=VM, scratch_shapes=[pltpu.VMEM((RANK,2*RANK),jnp.float32)],
        compiler_params=params(), name="factor")(gram)

def split(value):
    high = value.astype(jnp.bfloat16)
    return high, (value - high.astype(jnp.float32)).astype(jnp.bfloat16)

def right_kernel(raw_ref, inverse_ref, left_raw_ref, right_ref, squares_ref, left_ref):
    tile = 512
    inverse = inverse_ref[...]
    left_ref[...] = lax.dot_general(
        left_raw_ref[...], inverse, NT, precision=PRECISE, preferred_element_type=jnp.float32
    )
    high, low = split(inverse)
    factors = jnp.concatenate(
        [
            jnp.concatenate([high, high], axis=1),
            jnp.concatenate([low, jnp.zeros_like(low)], axis=1),
        ],
        axis=0,
    )
    total = jnp.zeros((8, RANK), jnp.float32)
    for at in range(0, raw_ref.shape[0], tile):
        both = jnp.concatenate(split(raw_ref[at : at + tile, :]), axis=1)
        out = lax.dot_general(both, factors, NT, preferred_element_type=jnp.float32)
        out = out[:, :RANK] + out[:, RANK:]
        right_ref[at : at + tile, :] = out
        total = total + jnp.sum((out * out).reshape(tile // 8, 8, RANK), axis=0)
    squares_ref[...] = jnp.sum(total, axis=0, keepdims=True)


def right_of(raw, inverse, left_raw):
    return pl.pallas_call(
        right_kernel,
        out_shape=(
            jax.ShapeDtypeStruct(raw.shape, jnp.float32),
            jax.ShapeDtypeStruct((1, RANK), jnp.float32),
            jax.ShapeDtypeStruct(left_raw.shape, jnp.float32),
        ),
        in_specs=[VM] * 3,
        out_specs=(VM, VM, VM),
        compiler_params=params(),
        name="right",
    )(raw, inverse, left_raw)


def update_kernel(
    decay, gain, right_ref, squares_ref, other_ref, left_ref, buffer_ref, weight_ref,
    weight_out, momentum_out, factor_out,
):
    tile = 512
    scale = lax.rsqrt((squares_ref[...] + other_ref[...]) + 1e-06)
    left = left_ref[...]
    high, low = split(jnp.concatenate([decay * left, (gain * left) * scale], axis=0))
    both_left = jnp.concatenate(
        [
            jnp.concatenate([high, high], axis=1),
            jnp.concatenate([low, jnp.zeros_like(low)], axis=1),
        ],
        axis=0,
    )
    n = left.shape[0]
    for at in range(0, right_ref.shape[0], tile):
        right = right_ref[at : at + tile, :]
        factor_out[at : at + tile, :] = right * scale
        both = jnp.concatenate(split(right), axis=1)
        out = lax.dot_general(both_left, both, NT, preferred_element_type=jnp.float32)
        out = out[: 2 * n] + out[2 * n :]
        momentum_out[:, at : at + tile] = buffer_ref[:, at : at + tile] - out[:n]
        weight_out[:, at : at + tile] = weight_ref[:, at : at + tile] - out[n:]


def update(decay, gain, right, squares, other, left, buffer, weight):
    return pl.pallas_call(
        functools.partial(update_kernel, decay, gain),
        out_shape=(
            jax.ShapeDtypeStruct(weight.shape, jnp.float32),
            jax.ShapeDtypeStruct(weight.shape, jnp.float32),
            jax.ShapeDtypeStruct(right.shape, jnp.float32),
        ),
        in_specs=[VM] * 6,
        out_specs=(VM, VM, VM),
        compiler_params=params(),
        name="update",
    )(right, squares, other, left, buffer, weight)


def gather(block, axis, size):
    return lax.all_to_all(
        jnp.broadcast_to(block[None], (size,) + block.shape), axis, 0, 0, tiled=True
    )


def packed(gram):
    half = RANK // 2
    corner = gram[half:, half:]
    corner = jnp.concatenate([corner[: half // 2], corner[half // 2 :]], axis=1)
    return jnp.concatenate([gram[:half], corner], axis=0)


def per_device(weight, momentum, grad, right_factor):
    rows, cols = momentum.shape
    near, far = X * B * B, J * K
    chunk = cols // near
    wide = -(-chunk // RANK) * RANK
    piece = chunk // far

    buffer = momentum + grad.astype(jnp.float32)
    left_raw = lax.psum(jnp.dot(buffer, right_factor, precision=PRECISE), "core")

    parts = buffer.reshape(rows, near, chunk).transpose(1, 0, 2)
    parts = jnp.pad(parts, ((0, 0), (0, 0), (0, wide - chunk)))
    sent = jnp.concatenate(
        [parts, jnp.broadcast_to(left_raw[None], (near, rows, RANK))], axis=2
    )
    held = lax.all_to_all(sent, NEAR, 0, 0, tiled=True).reshape(near * rows, wide + RANK)
    part = lax.dot_general(held, held[:, wide:], TN, precision=PRECISE)

    sent = jnp.concatenate(
        [
            part[:chunk].reshape(far, piece, RANK),
            packed(part[wide:]).reshape(far, -1, RANK),
        ],
        axis=1,
    )
    summed = jnp.sum(lax.all_to_all(sent, FAR, 0, 0, tiled=True), axis=0)

    by_far = gather(summed, FAR, far)
    gram = by_far[:, piece:].reshape(-1, RANK)
    right_raw = gather(by_far[:, :piece].reshape(chunk, RANK), NEAR, near).reshape(cols, RANK)
    right, squares, left = right_of(right_raw, factor(gram), left_raw)
    other = lax.ppermute(squares, "core", [(0, 1), (1, 0)])
    gain = 0.5 * math.sqrt(near * far * rows * 2 * cols / RANK)
    return update(1.0 - 0.95, gain, right, squares, other, left, buffer, weight)


def solution(mesh):
    dp = ("x", "yj", "yb", "zk", "zb")
    grid = Mesh(mesh.devices.reshape(X, J, B, K, B, 2), dp + ("core",))
    in_specs = (P(dp, "core"), P(dp, "core"), P(dp, "core"), P("core", None))
    out_specs = (P(dp, "core"), P(dp, "core"), P("core", None))
    return jax.shard_map(
        per_device, mesh=grid, in_specs=in_specs, out_specs=out_specs, check_vma=False
    )
```

time: 148 us -> 126 us (0.85)
  waiting for transfers between devices: 34 us -> 22 us
  local copies, waits for them, and re-layouts: 6.79 us -> 2.56 us
  blocking collectives: 74 us -> 71.7 us
  starting transfers between devices: 14.1 us -> 12 us
    all_to_all x1 -> x2, blocking collectives: 19.1 us -> 39.8 us  [the longest x1 29 us: per_device(): summed = jnp.sum(lax.all_to_all(sent, FAR, 0, 0, tiled=True), axis=0)]
    all_to_all x2 -> x1, blocking collectives: 37.9 us -> 19.2 us  [gather(): lax.all_to_all(jnp.broadcast_to(block[None], (size,) + block.shape), axis...]
    ppermute x3 -> x1, waiting for transfers between devices: 15.8 us -> 0.8 us  [per_device(): other = lax.ppermute(squares, 'core', [(0, 1), (1, 0)])]
    unnamed x14 -> x4, local copies, waits for them, and re-layouts: 5.62 us -> 0.39 us
    psum x1 -> x0, blocking collectives: 4.22 us -> none  [per_device(): squares = lax.psum(squares, 'core')]
    all_to_all x1, waiting for transfers between devices: 18.2 us -> 21.2 us  [gather(): lax.all_to_all(jnp.broadcast_to(block[None], (size,) + block.shape), axis...]
    ppermute x3 -> x1, starting transfers between devices: 8.27 us -> 6.04 us  [per_device(): other = lax.ppermute(squares, 'core', [(0, 1), (1, 0)])]
    broadcast_in_dim x2 -> x3, local copies, waits for them, and re-layouts: 0.06 us -> 1.66 us  [gather(): jnp.broadcast_to(block[None], (size,) + block.shape)]
  transfers between devices with their start and end apart: 4 -> 2, of which waited for: 2 -> 2; matrix products, arithmetic and copies ran while one was open for 0% -> 0% of each run, Pallas kernels for 5% -> 6%
where the time goes in v3:
time: 126 us
  blocking collectives  71.7 us (57%)
  waiting for transfers between devices  22 us (17%)
  Pallas kernels  12.9 us (10%)
  starting transfers between devices  12 us (10%)
  local copies, waits for them, and re-layouts  2.56 us (2%)
  matrix products  2.28 us (2%)
  other arithmetic  1.35 us (1%)
    all_to_all x1, blocking collectives, per_device(): summed = jnp.sum(lax.all_to_all(sent, FAR, 0, 0, tiled=True), axis=0)  29 us
    all_to_all x1, waiting for transfers between devices, gather(): lax.all_to_all(jnp.broadcast_to(block[None], (size,) + block.shape), axis...  21.2 us
    all_to_all x1, blocking collectives, gather(): lax.all_to_all(jnp.broadcast_to(block[None], (size,) + block.shape), axis...  19.2 us
    psum x1, blocking collectives, per_device(): lax.psum(jnp.dot(buffer, right_factor, precision=PRECISE), 'core')  12.7 us
    all_to_all x1, blocking collectives, per_device(): lax.all_to_all(sent, NEAR, 0, 0, tiled=True)  10.8 us
    pallas_call x1, Pallas kernels, factor(): pl.pallas_call(factor_kernel, out_shape=jax.ShapeDtypeStruct((RANK, RANK)...  7.84 us
    ppermute x1, starting transfers between devices, per_device(): other = lax.ppermute(squares, 'core', [(0, 1), (1, 0)])  6.04 us
    all_to_all x1, starting transfers between devices, gather(): lax.all_to_all(jnp.broadcast_to(block[None], (size,) + block.shape), axis...  5.97 us
  transfers between devices with their start and end apart: 2, of which 2 were waited for; matrix products, arithmetic and copies ran while one was open for 0% of the time, Pallas kernels for 6%

profile of v3, /device:TPU:1, one launch (start us, length us, event | category | flops | bytes accessed | tf_op | source)
XLA Modules:
  0.0 125.5 jit_solution(12974602879003161580)
XLA Ops:
  0.6 0.0 copy-start
  0.6 1.2 convert_add_fusion.buffer_ref
  1.8 0.3 reshape.27
  2.1 0.4 copy-done
  2.5 1.3 %fusion.3 = f32[16,128]{1,0:T(8,128)S(1)} fusion(f32[16,4608]{1,0:T(8,128)S(1)} %convert_add_fusion.buffer_ref, f32[4608,128]{1,0:T(8,128)S(1)} %copy-done), kind=kOutput, calls=%fused_computation.9 | convolution fusion | flops 113246208 | bytes 2662400 | tf_op jit(solution)/shard_map/dot_general | solution.py:169
  3.7 12.7 %psum.7.left_raw_ref = f32[16,128]{1,0:T(8,128)S(1)} all-reduce(f32[16,128]{1,0:T(8,128)S(1)} %fusion.3), channel_id=1, replica_groups=mesh['x'=4,'yj'=4,'yb'=2,'zk'=6,'zb'=2,'core'=2] {'core'}, use_global_device_ids=true, to_apply=%region_0.0 | all-reduce | flops 2048 | bytes 16384 | tf_op jit(solution)/shard_map/psum | solution.py:169
  16.4 0.1 copy.9
  16.6 10.8 %all_to_all.20 = f32[16,16,512]{2,1,0:T(8,128)S(1)} all-to-all(f32[16,16,512]{2,1,0:T(8,128)S(1)} %select_maximum_fusion), channel_id=1, replica_groups=mesh['x'=4,'yj'=4,'yb'=2,'zk'=6,'zb'=2,'core'=2] {'x','yb','zb'}, dimensions={0} | all-to-all | bytes 1048576 | tf_op jit(solution)/shard_map/all_to_all | solution.py:176
  27.4 1.0 fusion
  28.5 0.1 fusion.2
  28.6 0.1 maximum_maximum_fusion
  28.7 29.0 %all_to_all.21 = f32[24,16,128]{2,1,0:T(8,128)S(1)} all-to-all(f32[24,16,128]{2,1,0:T(8,128)S(1)} %pad_maximum_fusion), channel_id=1, replica_groups=mesh['x'=4,'yj'=4,'yb'=2,'zk'=6,'zb'=2,'core'=2] {'yj','zk'}, dimensions={0} | all-to-all | bytes 393216 | tf_op jit(solution)/shard_map/all_to_all | solution.py:186
  57.7 19.2 %all_to_all.22 = f32[24,16,128]{2,1,0:T(8,128)S(1)} all-to-all(f32[24,16,128]{2,1,0:T(8,128)S(1)} %broadcast_in_dim.9), channel_id=1, replica_groups=mesh['x'=4,'yj'=4,'yb'=2,'zk'=6,'zb'=2,'core'=2] {'yj','zk'}, dimensions={0} | all-to-all | bytes 393216 | tf_op jit(solution)/shard_map/all_to_all | solution.py:149
  76.9 1.6 %broadcast_in_dim.22 = f32[16,288,128]{2,1,0:T(8,128)} broadcast(f32[288,128]{1,0:T(8,128)S(1)} %broadcast_in_dim.10), dimensions={1,2} | broadcast | bytes 2506752 | tf_op jit(solution)/shard_map/broadcast_in_dim | solution.py:150
  78.6 6.0 %all-to-all-start.3 = ((f32[16,288,128]{2,1,0:T(8,128)}), f32[16,288,128]{2,1,0:T(8,128)}, u32[]{:S(2)}, u32[]{:S(2)}) async-start(f32[16,288,128]{2,1,0:T(8,128)} %broadcast_in_dim.22), calls=%async_computation.3 | async-start | bytes 4718592 | tf_op jit(solution)/shard_map/all_to_all | solution.py:149
  84.5 0.0 copy-start.1
  84.6 7.8 %factor.1.inverse_ref = f32[128,128]{1,0:T(8,128)S(1)} custom-call(f32[96,128]{1,0:T(8,128)S(1)} %bitcast.11), custom_call_target="tpu_custom_call" | custom-call | tf_op jit(solution)/shard_map/factor/pallas_call | solution.py:60
  92.4 21.2 %all-to-all-done.3 = f32[16,288,128]{2,1,0:T(8,128)} async-done(((f32[16,288,128]{2,1,0:T(8,128)}), f32[16,288,128]{2,1,0:T(8,128)}, u32[]{:S(2)}, u32[]{:S(2)}) %all-to-all-start.3) | async-done | bytes 2359328 | tf_op jit(solution)/shard_map/all_to_all | solution.py:149
  113.6 2.6 %right.1 = (f32[4608,128]{1,0:T(8,128)S(1)}, f32[1,128]{1,0:T(1,128)S(1)}, f32[16,128]{1,0:T(8,128)S(1)}) custom-call(f32[4608,128]{1,0:T(8,128)} %bitcast.3.raw_ref, f32[128,128]{1,0:T(8,128)S(1)} %factor.1.inverse_ref, f32[16,128]{1,0:T(8,128)S(1)} %psum.7.left_raw_ref), custom_call_target="tpu_custom_call" | custom-call | tf_op jit(solution)/shard_map/right/pallas_call | solution.py:93
  116.2 6.0 %collective-permute-start = (f32[1,128]{1,0:T(1,128)S(1)}, f32[1,128]{1,0:T(1,128)S(1)}, u32[]{:S(2)}, u32[]{:S(2)}) collective-permute-start(f32[1,128]{1,0:T(1,128)S(1)} %get-tuple-element.7.squares_ref), channel_id=1, source_target_pairs={{0,1},{1,0},{2,3},{3,2},{4,5},{5,4},{6,7},{7,6},{8,9},{9,8},{10,11... | collective-permute-start | bytes 1544 | tf_op jit(solution)/shard_map/ppermute | solution.py:192
  122.3 0.8 collective-permute-done.other_ref
  123.1 0.0 copy-done.1
  123.1 2.5 %update.1 = (f32[16,4608]{1,0:T(8,128)}, f32[16,4608]{1,0:T(8,128)}, f32[4608,128]{1,0:T(8,128)}) custom-call(f32[4608,128]{1,0:T(8,128)S(1)} %get-tuple-element.6.right_ref, f32[1,128]{1,0:T(1,128)S(1)} %get-tuple-element.7.squares_ref, f32[1,128]{1,0:T(1,128)S(1)} %collective-permute-done.other_ref, f32[16,128]{1,0:T(8,128)S(1)} %get-tuple-element.8.left_ref, ...), custom_call_target="tpu_custom_call" | custom-call | tf_op jit(solution)/shard_map/update/pallas_call | solution.py:134
  (10 shorter events, 0.2 us)
Async XLA Ops:
  0.6 1.8 %copy-start = (f32[4608,128]{1,0:T(8,128)S(1)}, f32[4608,128]{1,0:T(8,128)}, u32[]{:S(2)}) copy-start(f32[4608,128]{1,0:T(8,128)} %param.7) | copy-start | bytes 7077892
  78.6 35.1 %all-to-all-start.3 = ((f32[16,288,128]{2,1,0:T(8,128)}), f32[16,288,128]{2,1,0:T(8,128)}, u32[]{:S(2)}, u32[]{:S(2)}) async-start(f32[16,288,128]{2,1,0:T(8,128)} %broadcast_in_dim.22), calls=%async_computation.3 | async-start | bytes 4718592 | tf_op jit(solution)/shard_map/all_to_all | solution.py:149
  84.5 38.5 %copy-start.1 = (f32[16,4608]{1,0:T(8,128)S(1)}, f32[16,4608]{1,0:T(8,128)}, u32[]{:S(2)}) copy-start(f32[16,4608]{1,0:T(8,128)} %weight_ref.1) | copy-start | bytes 884740
  116.2 6.8 %collective-permute-start = (f32[1,128]{1,0:T(1,128)S(1)}, f32[1,128]{1,0:T(1,128)S(1)}, u32[]{:S(2)}, u32[]{:S(2)}) collective-permute-start(f32[1,128]{1,0:T(1,128)S(1)} %get-tuple-element.7.squares_ref), channel_id=1, source_target_pairs={{0,1},{1,0},{2,3},{3,2},{4,5},{5,4},{6,7},{7,6},{8,9},{9,8},{10,11... | collective-permute-start | bytes 1544 | tf_op jit(solution)/shard_map/ppermute | solution.py:192

commit v4 on v0

v4 whole, which is shorter than its diff:
```python
import functools
import math

import jax
import jax.numpy as jnp
from jax import lax
from jax.experimental import pallas as pl
from jax.experimental.pallas import tpu as pltpu
from jax.sharding import PartitionSpec as P

PRECISE = lax.Precision.HIGHEST
X, Y, Z = 4, 8, 12
ALL = ("dp", "tensor")
RANK = 128
NT = (((1,), (1,)), ((), ()))
TN = (((0,), (0,)), ((), ()))
VM = pl.BlockSpec(memory_space=pltpu.VMEM)
SM = pl.BlockSpec(memory_space=pltpu.SMEM)


def params():
    return pltpu.CompilerParams(vmem_limit_bytes=16 * 1024 * 1024)


def split(value, parts=2):
    out = []
    for _ in range(parts):
        out.append(value.astype(jnp.bfloat16))
        value = value - out[-1].astype(jnp.float32)
    return out


def inverse_factor(gram, store):
    step = 16
    row = lax.broadcasted_iota(jnp.int32, (RANK, RANK), 0)
    col = lax.broadcasted_iota(jnp.int32, (RANK, RANK), 1)
    rest = jnp.concatenate([gram, (row == col).astype(jnp.float32)], axis=1)
    for at in range(0, RANK, step):
        rows = [rest[i : i + 1, :] for i in range(step)]
        corner = rest[:step, at : at + step]
        entry = {
            (i, j): jnp.broadcast_to(corner[i : i + 1, j : j + 1], (1, RANK))
            for i in range(step)
            for j in range(i, step)
        }
        for i in range(step):
            scale = lax.rsqrt(entry[i, i])
            pivot = {j: entry[i, j] * scale for j in range(i + 1, step)}
            rows[i] = rows[i] * jnp.concatenate([scale, scale], axis=1)
            for j in range(i + 1, step):
                rows[j] = rows[j] - jnp.concatenate([pivot[j], pivot[j]], axis=1) * rows[i]
                for k in range(j, step):
                    entry[j, k] = entry[j, k] - pivot[j] * pivot[k]
        done = jnp.concatenate(rows, axis=0)
        store(at, done[:, RANK:])
        if at + step < RANK:
            l1, l2, l3 = split(done[:, :RANK], 3)
            r1, r2, r3 = split(done, 3)
            change = lax.dot_general(
                jnp.concatenate([l1, l1, l2, l2, l1, l3], axis=0),
                jnp.concatenate([r1, r2, r1, r2, r3, r1], axis=0),
                TN,
                preferred_element_type=jnp.float32,
            )
            rest = rest[step:] - change[at + step :]


def factor_kernel(packed_ref, inverse_ref):
    half = RANK // 2
    rest = packed_ref[half:, :]
    nothing = jnp.zeros((half // 2, half), jnp.float32)
    gram = jnp.concatenate(
        [
            packed_ref[:half, :],
            jnp.concatenate([nothing, rest[:, :half]], axis=1),
            jnp.concatenate([nothing, rest[:, half:]], axis=1),
        ],
        axis=0,
    )

    def store(at, rows):
        inverse_ref[at : at + rows.shape[0], :] = rows

    inverse_factor(gram, store)


def factor(packed_gram):
    return pl.pallas_call(
        factor_kernel,
        out_shape=jax.ShapeDtypeStruct((RANK, RANK), jnp.float32),
        in_specs=[VM],
        out_specs=VM,
        compiler_params=params(),
        name="factor",
    )(packed_gram)


def right_kernel(at_ref, own_ref, other_ref, inverse_ref, left_raw_ref, right_ref, squares_ref, left_ref):
    rows = own_ref.shape[0]
    inverse = inverse_ref[...]
    left_ref[...] = lax.dot_general(
        left_raw_ref[...], inverse, NT, precision=PRECISE, preferred_element_type=jnp.float32
    )
    squares = jnp.zeros((8, RANK), jnp.float32)
    for place, raw in ((at_ref[0], own_ref), (1 - at_ref[0], other_ref)):
        right = lax.dot_general(
            raw[...], inverse, NT, precision=PRECISE, preferred_element_type=jnp.float32
        )
        right_ref[pl.ds(pl.multiple_of(place * rows, 8), rows), :] = right
        squares = squares + jnp.sum((right * right).reshape(-1, 8, RANK), axis=0)
    squares_ref[...] = squares


def right_of(at, own, other, inverse, left_raw):
    return pl.pallas_call(
        right_kernel,
        out_shape=(
            jax.ShapeDtypeStruct((2 * own.shape[0], RANK), jnp.float32),
            jax.ShapeDtypeStruct((8, RANK), jnp.float32),
            jax.ShapeDtypeStruct(left_raw.shape, jnp.float32),
        ),
        in_specs=[SM] + [VM] * 4,
        out_specs=(VM, VM, VM),
        compiler_params=params(),
        name="right",
    )(at, own, other, inverse, left_raw)


def update_kernel(
    decay, gain, right_ref, left_ref, buffer_ref, weight_ref, weight_out, momentum_out, factor_out
):
    near, pitch, _ = right_ref.shape
    chunk, group = pitch - 8, 2
    squares = right_ref[0, chunk:, :]
    for k in range(1, near):
        squares = squares + right_ref[k, chunk:, :]
    scale = lax.rsqrt(jnp.sum(squares, axis=0, keepdims=True) + 1e-06)
    left = left_ref[...]
    high, low = split(jnp.concatenate([decay * left, (gain * left) * scale], axis=0))
    both_left = jnp.concatenate(
        [
            jnp.concatenate([high, high], axis=1),
            jnp.concatenate([low, jnp.zeros_like(low)], axis=1),
        ],
        axis=0,
    )
    n = left.shape[0]
    for first in range(0, near, group):
        right = jnp.concatenate([right_ref[first + k, :chunk, :] for k in range(group)], axis=0)
        at, end = first * chunk, (first + group) * chunk
        factor_out[at:end, :] = right * scale
        both = jnp.concatenate(split(right), axis=1)
        out = lax.dot_general(both_left, both, NT, preferred_element_type=jnp.float32)
        out = out[: 2 * n] + out[2 * n :]
        momentum_out[:, at:end] = buffer_ref[:, at:end] - out[:n]
        weight_out[:, at:end] = weight_ref[:, at:end] - out[n:]


def update(decay, gain, right, left, buffer, weight):
    return pl.pallas_call(
        functools.partial(update_kernel, decay, gain),
        out_shape=(
            jax.ShapeDtypeStruct(weight.shape, jnp.float32),
            jax.ShapeDtypeStruct(weight.shape, jnp.float32),
            jax.ShapeDtypeStruct((weight.shape[1], RANK), jnp.float32),
        ),
        in_specs=[VM] * 4,
        out_specs=(VM, VM, VM),
        compiler_params=params(),
        name="update",
    )(right, left, buffer, weight)


def groups(same, order):
    found = {}
    for device in range(X * Y * Z * 2):
        chip, core = divmod(device, 2)
        x, y, z = shifted(chip, core)
        found.setdefault((core, same(x, y, z)), []).append((order(x, y, z), device))
    return [[device for _, device in sorted(members)] for members in found.values()]


def shifted(chip, core):
    return (chip // (Y * Z) + core) % X, (chip // Z % Y + core) % Y, (chip % Z + core) % Z


def cube(x, y, z):
    return x % 2, y % 2, z % 2


def far(x, y, z):
    return y // 2, z // 2


CUBE = groups(lambda x, y, z: (x // 2, y // 2, z // 2), cube)
NEAR = groups(far, lambda x, y, z: cube(x, y, z) + (x // 2,))
FAR = groups(lambda x, y, z: cube(x, y, z) + (x // 2,), far)


def exchange(blocks, members):
    return lax.all_to_all(blocks, ALL, 0, 0, axis_index_groups=members, tiled=True)


def gather(block, members):
    return exchange(jnp.broadcast_to(block[None], (len(members[0]),) + block.shape), members)


def packed(gram):
    half = RANK // 2
    corner = gram[half:, half:]
    corner = jnp.concatenate([corner[: half // 2], corner[half // 2 :]], axis=1)
    return jnp.concatenate([gram[:half], corner], axis=0)


def per_device(weight, momentum, grad, right_factor):
    rows, cols = momentum.shape
    n_near, n_far = len(NEAR[0]), len(FAR[0])
    chunk = cols // n_near
    wide = -(-chunk // RANK) * RANK
    piece = chunk // n_far

    buffer = momentum + grad.astype(jnp.float32)
    left_raw = lax.psum(jnp.dot(buffer, right_factor, precision=PRECISE), "tensor")

    parts = buffer.reshape(rows, n_near, chunk).transpose(1, 0, 2)
    parts = jnp.pad(parts, ((0, 0), (0, 0), (0, wide - chunk)))
    beside = jnp.broadcast_to(left_raw[None], (n_near, rows, RANK))
    held = exchange(jnp.concatenate([parts, beside], axis=2), NEAR)
    held = held.reshape(n_near * rows, wide + RANK)
    part = lax.dot_general(held, held[:, wide:], TN, precision=PRECISE)

    sent = jnp.concatenate(
        [
            part[:chunk].reshape(n_far, piece, RANK),
            packed(part[wide:]).reshape(n_far, -1, RANK),
        ],
        axis=1,
    )
    summed = jnp.sum(exchange(sent, FAR), axis=0)

    by_far = gather(summed, FAR)
    own = by_far[:, :piece].reshape(chunk, RANK)
    count = X * Y * Z
    other = lax.ppermute(own, "dp", [(i, (i + count // 2) % count) for i in range(count)])
    inverse = factor(by_far[:, piece:].reshape(-1, RANK))
    x = (lax.axis_index("dp") // (Y * Z) + lax.axis_index("tensor")) % X
    right, squares, left = right_of((x // 2).reshape(1), own, other, inverse, left_raw)
    squares = lax.psum(squares, "tensor")
    by_cube = gather(jnp.concatenate([right, squares], axis=0), CUBE)
    gain = 0.5 * math.sqrt(count * rows * 2 * cols / RANK)
    return update(1.0 - 0.95, gain, by_cube, left, buffer, weight)


def solution(mesh):
    in_specs = (P("dp", "tensor"), P("dp", "tensor"), P("dp", "tensor"), P("tensor", None))
    out_specs = (P("dp", "tensor"), P("dp", "tensor"), P("tensor", None))
    return jax.shard_map(
        per_device, mesh=mesh, in_specs=in_specs, out_specs=out_specs, check_vma=False
    )
```

time: 841 us -> 121 us (0.14)
  waiting for transfers between devices: 760 us -> 0.01 us
  blocking collectives: 22 us -> 103 us
  other arithmetic: 27.9 us -> 1.37 us
  between operations: 14.1 us -> 0.84 us
  matrix products: 14.1 us -> 2.26 us
    psum x2 -> x0, waiting for transfers between devices: 760 us -> none  [the longest x1 394 us: per_device(): right = lax.psum(jnp.dot(buffer.T, left, precision=PRECISE), 'dp')]
    all_to_all x0 -> x4, blocking collectives: none -> 84.3 us  [exchange(): lax.all_to_all(blocks, ALL, 0, 0, axis_index_groups=members, tiled=True)]
    another operation x5 -> x0, other arithmetic: 22.9 us -> none  [the longest x3 12.4 us: per_device(): lower_factor = jnp.linalg.cholesky(gram)]
    dot_general x4 -> x1, matrix products: 11.7 us -> 0.99 us  [per_device(): part = lax.dot_general(held, held[:, wide:], TN, precision=PRECISE)]
  transfers between devices with their start and end apart: 2 -> 1, of which waited for: 2 -> 0; matrix products, arithmetic and copies ran while one was open for 0% -> 0% of each run, Pallas kernels for 0% -> 4%
where the time goes in v4:
time: 121 us
  blocking collectives  103 us (85%)
  Pallas kernels  7.9 us (7%)
  starting transfers between devices  4.34 us (4%)
  matrix products  2.26 us (2%)
  other arithmetic  1.37 us (1%)
    all_to_all x4, blocking collectives, exchange(): lax.all_to_all(blocks, ALL, 0, 0, axis_index_groups=members, tiled=True)  84.3 us
    psum x1, blocking collectives, per_device(): lax.psum(jnp.dot(buffer, right_factor, precision=PRECISE), 'tensor')  12.7 us
    psum x1, blocking collectives, per_device(): squares = lax.psum(squares, 'tensor')  5.96 us
    pallas_call x1, Pallas kernels, factor(): pl.pallas_call(factor_kernel, out_shape=jax.ShapeDtypeStruct((RANK, RANK)...  4.93 us
    ppermute x1, starting transfers between devices, per_device(): lax.ppermute(own, 'dp', [(i, (i + count // 2) % count) for i in range(cou...  4.34 us
    pallas_call x1, Pallas kernels, update(): pl.pallas_call(functools.partial(update_kernel, decay, gain), out_shape=(...  2.45 us
  transfers between devices with their start and end apart: 1, of which 0 were waited for; matrix products, arithmetic and copies ran while one was open for 0% of the time, Pallas kernels for 4%

profile of v4, /device:TPU:1, one launch (start us, length us, event | category | flops | bytes accessed | tf_op | source)
XLA Modules:
  0.0 120.7 jit_solution(2748045484780179593)
XLA Ops:
  0.6 0.0 copy-start
  0.6 1.2 convert_add_fusion.buffer_ref
  1.8 0.3 reshape.31
  2.1 0.4 copy-done
  2.5 1.3 %fusion.3 = f32[16,128]{1,0:T(8,128)S(1)} fusion(f32[16,4608]{1,0:T(8,128)S(1)} %convert_add_fusion.buffer_ref, f32[4608,128]{1,0:T(8,128)S(1)} %copy-done), kind=kOutput, calls=%fused_computation.10 | convolution fusion | flops 113246208 | bytes 2662400 | tf_op jit(solution)/shard_map/dot_general | solution.py:223
  3.7 12.7 %psum.14.left_raw_ref = f32[16,128]{1,0:T(8,128)S(1)} all-reduce(f32[16,128]{1,0:T(8,128)S(1)} %fusion.3), channel_id=1, replica_groups=mesh['dp'=384,'tensor'=2] {'tensor'}, use_global_device_ids=true, to_apply=%region_0.0 | all-reduce | flops 2048 | bytes 16384 | tf_op jit(solution)/shard_map/psum | solution.py:223
  16.4 0.1 copy.9
  16.6 15.9 %all_to_all.20 = f32[16,16,512]{2,1,0:T(8,128)S(1)} all-to-all(f32[16,16,512]{2,1,0:T(8,128)S(1)} %select_maximum_fusion), channel_id=1, replica_groups={{0,384,2,386,24,408,26,410,192,576,194,578,216,600,218,602},{767,383,74..., dimensions={0} | all-to-all | bytes 1048576 | tf_op jit(solution)/shard_map/all_to_all | solution.py:201
  32.5 1.0 fusion
  33.5 0.1 fusion.2
  33.7 0.1 maximum_maximum_fusion
  33.8 25.8 %all_to_all.21 = f32[24,16,128]{2,1,0:T(8,128)S(1)} all-to-all(f32[24,16,128]{2,1,0:T(8,128)S(1)} %pad_maximum_fusion.1), channel_id=1, replica_groups={{0,4,8,12,16,20,48,52,56,60,64,68,96,100,104,108,112,116,144,148,152,15..., dimensions={0} | all-to-all | bytes 393216 | tf_op jit(solution)/shard_map/all_to_all | solution.py:201
  59.7 19.9 %all_to_all.22 = f32[24,16,128]{2,1,0:T(8,128)S(1)} all-to-all(f32[24,16,128]{2,1,0:T(8,128)S(1)} %broadcast_in_dim.7), channel_id=1, replica_groups={{0,4,8,12,16,20,48,52,56,60,64,68,96,100,104,108,112,116,144,148,152,15..., dimensions={0} | all-to-all | bytes 393216 | tf_op jit(solution)/shard_map/all_to_all | solution.py:201
  79.6 4.3 %collective-permute-start = (f32[288,128]{1,0:T(8,128)S(1)}, f32[288,128]{1,0:T(8,128)S(1)}, u32[]{:S(2)}, u32[]{:S(2)}) collective-permute-start(f32[288,128]{1,0:T(8,128)S(1)} %reshape.35.own_ref), channel_id=1, source_target_pairs={{0,384},{2,386},{4,388},{6,390},{8,392},{10,394},{12,396},{14,398}... | collective-permute-start | bytes 442376 | tf_op jit(solution)/shard_map/ppermute | solution.py:244
  84.0 4.9 %factor.1.inverse_ref = f32[128,128]{1,0:T(8,128)S(1)} custom-call(f32[96,128]{1,0:T(8,128)S(1)} %bitcast.11), custom_call_target="tpu_custom_call" | custom-call | tf_op jit(solution)/shard_map/factor/pallas_call | solution.py:88
  88.9 0.0 collective-permute-done.other_ref
  88.9 0.5 right.1
  89.5 6.0 %psum.15 = f32[8,128]{1,0:T(8,128)S(1)} all-reduce(f32[8,128]{1,0:T(8,128)S(1)} %get-tuple-element.7), channel_id=1, replica_groups=mesh['dp'=384,'tensor'=2] {'tensor'}, use_global_device_ids=true, to_apply=%region_2.3 | all-reduce | flops 1024 | bytes 8192 | tf_op jit(solution)/shard_map/psum | solution.py:248
  95.4 0.2 broadcast_in_dim.8
  95.6 0.0 copy-start.1
  95.6 22.6 %all_to_all.23.right_ref = f32[8,584,128]{2,1,0:T(8,128)S(1)} all-to-all(f32[8,584,128]{2,1,0:T(8,128)S(1)} %broadcast_in_dim.8), channel_id=1, replica_groups={{0,2,24,26,192,194,216,218},{767,745,599,577,191,169,23,1},{747,749,579..., dimensions={0} | all-to-all | bytes 4784128 | tf_op jit(solution)/shard_map/all_to_all | solution.py:201
  118.2 0.0 copy-done.1
  118.2 2.5 %update.1 = (f32[16,4608]{1,0:T(8,128)}, f32[16,4608]{1,0:T(8,128)}, f32[4608,128]{1,0:T(8,128)}) custom-call(f32[8,584,128]{2,1,0:T(8,128)S(1)} %all_to_all.23.right_ref, f32[16,128]{1,0:T(8,128)S(1)} %get-tuple-element.8.left_ref, f32[16,4608]{1,0:T(8,128)S(1)} %convert_add_fusion.buffer_ref, f32[16,4608]{1,0:T(8,128)S(1)} %copy-done.1), custom_call_target="tpu_custom_call" | custom-call | tf_op jit(solution)/shard_map/update/pallas_call | solution.py:160
  (11 shorter events, 0.2 us)
Async XLA Ops:
  0.6 1.8 %copy-start = (f32[4608,128]{1,0:T(8,128)S(1)}, f32[4608,128]{1,0:T(8,128)}, u32[]{:S(2)}) copy-start(f32[4608,128]{1,0:T(8,128)} %param.7) | copy-start | bytes 7077892
  79.6 9.4 %collective-permute-start = (f32[288,128]{1,0:T(8,128)S(1)}, f32[288,128]{1,0:T(8,128)S(1)}, u32[]{:S(2)}, u32[]{:S(2)}) collective-permute-start(f32[288,128]{1,0:T(8,128)S(1)} %reshape.35.own_ref), channel_id=1, source_target_pairs={{0,384},{2,386},{4,388},{6,390},{8,392},{10,394},{12,396},{14,398}... | collective-permute-start | bytes 442376 | tf_op jit(solution)/shard_map/ppermute | solution.py:244
  95.6 22.6 %copy-start.1 = (f32[16,4608]{1,0:T(8,128)S(1)}, f32[16,4608]{1,0:T(8,128)}, u32[]{:S(2)}) copy-start(f32[16,4608]{1,0:T(8,128)} %weight_ref.1) | copy-start | bytes 884740

commit v5 on v4

--- a/solution.py
+++ b/solution.py
@@ -16,6 +16,7 @@
 TN = (((0,), (0,)), ((), ()))
 VM = pl.BlockSpec(memory_space=pltpu.VMEM)
 SM = pl.BlockSpec(memory_space=pltpu.SMEM)
+ANY = pl.BlockSpec(memory_space=pl.ANY)
 
 
 def params():
@@ -28,6 +29,68 @@
         out.append(value.astype(jnp.bfloat16))
         value = value - out[-1].astype(jnp.float32)
     return out
+
+
+def head_kernel(buffer_ref, factor_ref, parts_ref, left_ref):
+    n_parts, rows, wide = parts_ref.shape
+    chunk = buffer_ref.shape[1] // n_parts
+    zeros = jnp.zeros((rows, wide - chunk), jnp.float32)
+    for k in range(n_parts):
+        part = buffer_ref[:, k * chunk : (k + 1) * chunk]
+        parts_ref[k, :, :] = jnp.concatenate([part, zeros], axis=1)
+    b1, b2 = split(buffer_ref[...])
+    f1, f2 = split(factor_ref[...])
+    both = jnp.dot(jnp.concatenate([b1, b2], axis=0), f1, preferred_element_type=jnp.float32)
+    small = both[rows:] + jnp.dot(b1, f2, preferred_element_type=jnp.float32)
+    left_ref[...] = small + both[:rows]
+
+
+def head(buffer, right_factor, n_parts, wide):
+    rows = buffer.shape[0]
+    return pl.pallas_call(
+        head_kernel,
+        out_shape=(
+            jax.ShapeDtypeStruct((n_parts, rows, wide), jnp.float32),
+            jax.ShapeDtypeStruct((rows, RANK), jnp.float32),
+        ),
+        in_specs=[VM, VM],
+        out_specs=(VM, VM),
+        compiler_params=params(),
+        name="head",
+    )(buffer, right_factor)
+
+
+def part_kernel(piece, held_ref, sent_ref, part):
+    n, pitch, _ = sent_ref.shape
+    wide, share, half = held_ref.shape[1] - RANK, pitch - piece, RANK // 2
+    h1, h2 = split(held_ref[...])
+    l1, l2 = h1[:, wide:], h2[:, wide:]
+    product = lax.dot_general(
+        jnp.concatenate([h2, h1, h1], axis=0),
+        jnp.concatenate([l1, l2, l1], axis=0),
+        TN,
+        preferred_element_type=jnp.float32,
+    )
+    part[...] = product[: n * piece]
+    corner = product[wide + half :, half:]
+    corner = jnp.concatenate([corner[: half // 2], corner[half // 2 :]], axis=1)
+    packed = jnp.concatenate([product[wide : wide + half], corner], axis=0)
+    for k in range(n):
+        sent_ref[k, :piece, :] = part[k * piece : (k + 1) * piece, :]
+        sent_ref[k, piece:, :] = packed[k * share : (k + 1) * share, :]
+
+
+def part_of(held, n, piece):
+    share = (RANK // 2 + RANK // 4) // n
+    return pl.pallas_call(
+        functools.partial(part_kernel, piece),
+        out_shape=jax.ShapeDtypeStruct((n, piece + share, RANK), jnp.float32),
+        in_specs=[VM],
+        out_specs=VM,
+        scratch_shapes=[pltpu.VMEM((n * piece, RANK), jnp.float32)],
+        compiler_params=params(),
+        name="part",
+    )(held)
 
 
 def inverse_factor(gram, store):
@@ -127,7 +190,8 @@
 
 
 def update_kernel(
-    decay, gain, right_ref, left_ref, buffer_ref, weight_ref, weight_out, momentum_out, factor_out
+    decay, gain, right_ref, left_ref, buffer_ref, weight_ref, weight_out, momentum_out, factor_out,
+    weight_new, momentum_new, factor_new, sent,
 ):
     near, pitch, _ = right_ref.shape
     chunk, group = pitch - 8, 2
@@ -145,27 +209,40 @@
         axis=0,
     )
     n = left.shape[0]
+    copies = []
+
+    def send(source, target):
+        copies.append(pltpu.make_async_copy(source, target, sent.at[len(copies)]))
+        copies[-1].start()
+
     for first in range(0, near, group):
+        for k in range(first, first + group):
+            factor_new[k * chunk : (k + 1) * chunk, :] = right_ref[k, :chunk, :] * scale
+        at, end = first * chunk, (first + group) * chunk
+        send(factor_new.at[at:end, :], factor_out.at[at:end, :])
+    for first in range(0, near, group):
+        at, end = first * chunk, (first + group) * chunk
         right = jnp.concatenate([right_ref[first + k, :chunk, :] for k in range(group)], axis=0)
-        at, end = first * chunk, (first + group) * chunk
-        factor_out[at:end, :] = right * scale
         both = jnp.concatenate(split(right), axis=1)
         out = lax.dot_general(both_left, both, NT, preferred_element_type=jnp.float32)
         out = out[: 2 * n] + out[2 * n :]
-        momentum_out[:, at:end] = buffer_ref[:, at:end] - out[:n]
-        weight_out[:, at:end] = weight_ref[:, at:end] - out[n:]
+        momentum_new[:, at:end] = buffer_ref[:, at:end] - out[:n]
+        weight_new[:, at:end] = weight_ref[:, at:end] - out[n:]
+        send(momentum_new.at[:, at:end], momentum_out.at[:, at:end])
+        send(weight_new.at[:, at:end], weight_out.at[:, at:end])
+    for copy in copies:
+        copy.wait()
 
 
 def update(decay, gain, right, left, buffer, weight):
+    shapes = (weight.shape, weight.shape, (weight.shape[1], RANK))
     return pl.pallas_call(
         functools.partial(update_kernel, decay, gain),
-        out_shape=(
-            jax.ShapeDtypeStruct(weight.shape, jnp.float32),
-            jax.ShapeDtypeStruct(weight.shape, jnp.float32),
-            jax.ShapeDtypeStruct((weight.shape[1], RANK), jnp.float32),
-        ),
+        out_shape=tuple(jax.ShapeDtypeStruct(shape, jnp.float32) for shape in shapes),
         in_specs=[VM] * 4,
-        out_specs=(VM, VM, VM),
+        out_specs=(ANY,) * 3,
+        scratch_shapes=[pltpu.VMEM(shape, jnp.float32) for shape in shapes]
+        + [pltpu.SemaphoreType.DMA((12,))],
         compiler_params=params(),
         name="update",
     )(right, left, buffer, weight)
@@ -205,13 +282,6 @@
     return exchange(jnp.broadcast_to(block[None], (len(members[0]),) + block.shape), members)
 
 
-def packed(gram):
-    half = RANK // 2
-    corner = gram[half:, half:]
-    corner = jnp.concatenate([corner[: half // 2], corner[half // 2 :]], axis=1)
-    return jnp.concatenate([gram[:half], corner], axis=0)
-
-
 def per_device(weight, momentum, grad, right_factor):
     rows, cols = momentum.shape
     n_near, n_far = len(NEAR[0]), len(FAR[0])
@@ -220,22 +290,12 @@
     piece = chunk // n_far
 
     buffer = momentum + grad.astype(jnp.float32)
-    left_raw = lax.psum(jnp.dot(buffer, right_factor, precision=PRECISE), "tensor")
-
-    parts = buffer.reshape(rows, n_near, chunk).transpose(1, 0, 2)
-    parts = jnp.pad(parts, ((0, 0), (0, 0), (0, wide - chunk)))
+    parts, left_part = head(buffer, right_factor, n_near, wide)
+    left_raw = lax.psum(left_part, "tensor")
     beside = jnp.broadcast_to(left_raw[None], (n_near, rows, RANK))
     held = exchange(jnp.concatenate([parts, beside], axis=2), NEAR)
-    held = held.reshape(n_near * rows, wide + RANK)
-    part = lax.dot_general(held, held[:, wide:], TN, precision=PRECISE)
-
-    sent = jnp.concatenate(
-        [
-            part[:chunk].reshape(n_far, piece, RANK),
-            packed(part[wide:]).reshape(n_far, -1, RANK),
-        ],
-        axis=1,
-    )
+
+    sent = part_of(held.reshape(n_near * rows, wide + RANK), n_far, piece)
     summed = jnp.sum(exchange(sent, FAR), axis=0)
 
     by_far = gather(summed, FAR)

time: 121 us -> 120 us (level)
  matrix products: 2.26 us -> 0 us
    dot_general x2 -> x0, matrix products: 2.26 us -> none  [the longest x1 1.27 us: per_device(): jnp.dot(buffer, right_factor, precision=PRECISE)]
    unnamed x4, local copies, waits for them, and re-layouts: 0.39 us -> 1.67 us
    pallas_call x1 -> x3, Pallas kernels: 2.45 us -> 3.06 us  [the longest x1 2.02 us: update(): pl.pallas_call(functools.partial(update_kernel, decay, gain), out_shape=t...]
where the time goes in v5:
time: 120 us
  blocking collectives  103 us (86%)
  Pallas kernels  8.51 us (7%)
  starting transfers between devices  4.35 us (4%)
  local copies, waits for them, and re-layouts  1.88 us (2%)
    all_to_all x4, blocking collectives, exchange(): lax.all_to_all(blocks, ALL, 0, 0, axis_index_groups=members, tiled=True)  84.2 us
    psum x1, blocking collectives, per_device(): left_raw = lax.psum(left_part, 'tensor')  12.7 us
    psum x1, blocking collectives, per_device(): squares = lax.psum(squares, 'tensor')  5.96 us
    pallas_call x1, Pallas kernels, factor(): pl.pallas_call(factor_kernel, out_shape=jax.ShapeDtypeStruct((RANK, RANK)...  4.93 us
    ppermute x1, starting transfers between devices, per_device(): lax.ppermute(own, 'dp', [(i, (i + count // 2) % count) for i in range(cou...  4.35 us
  transfers between devices with their start and end apart: 1, of which 0 were waited for; matrix products, arithmetic and copies ran while one was open for 0% of the time, Pallas kernels for 4%

profile of v5, /device:TPU:1, one launch (start us, length us, event | category | flops | bytes accessed | tf_op | source)
XLA Modules:
  0.0 119.5 jit_solution(6153347554630780335)
XLA Ops:
  0.6 1.0 convert_add_fusion.buffer_ref
  1.7 0.0 copy-start
  1.7 1.7 %copy-done = f32[4608,128]{1,0:T(8,128)S(1)} copy-done((f32[4608,128]{1,0:T(8,128)S(1)}, f32[4608,128]{1,0:T(8,128)}, u32[]{:S(2)}) %copy-start) | copy-done | bytes 2359320
  3.3 0.6 head.1
  3.9 12.7 %psum.14.left_raw_ref = f32[16,128]{1,0:T(8,128)S(1)} all-reduce(f32[16,128]{1,0:T(8,128)S(1)} %get-tuple-element.9), channel_id=1, replica_groups=mesh['dp'=384,'tensor'=2] {'tensor'}, use_global_device_ids=true, to_apply=%region_0.0 | all-reduce | flops 2048 | bytes 16384 | tf_op jit(solution)/shard_map/psum | solution.py:294
  16.6 15.9 %all_to_all.20 = f32[16,16,512]{2,1,0:T(8,128)S(1)} all-to-all(f32[16,16,512]{2,1,0:T(8,128)S(1)} %pad_maximum_fusion), channel_id=1, replica_groups={{0,384,2,386,24,408,26,410,192,576,194,578,216,600,218,602},{767,383,74..., dimensions={0} | all-to-all | bytes 1048576 | tf_op jit(solution)/shard_map/all_to_all | solution.py:278
  32.5 0.5 part.1
  33.0 25.8 %all_to_all.21 = f32[24,16,128]{2,1,0:T(8,128)S(1)} all-to-all(f32[24,16,128]{2,1,0:T(8,128)S(1)} %part.1), channel_id=1, replica_groups={{0,4,8,12,16,20,48,52,56,60,64,68,96,100,104,108,112,116,144,148,152,15..., dimensions={0} | all-to-all | bytes 393216 | tf_op jit(solution)/shard_map/all_to_all | solution.py:278
  58.9 19.9 %all_to_all.22 = f32[24,16,128]{2,1,0:T(8,128)S(1)} all-to-all(f32[24,16,128]{2,1,0:T(8,128)S(1)} %broadcast_in_dim.7), channel_id=1, replica_groups={{0,4,8,12,16,20,48,52,56,60,64,68,96,100,104,108,112,116,144,148,152,15..., dimensions={0} | all-to-all | bytes 393216 | tf_op jit(solution)/shard_map/all_to_all | solution.py:278
  78.8 4.3 %collective-permute-start = (f32[288,128]{1,0:T(8,128)S(1)}, f32[288,128]{1,0:T(8,128)S(1)}, u32[]{:S(2)}, u32[]{:S(2)}) collective-permute-start(f32[288,128]{1,0:T(8,128)S(1)} %reshape.23.own_ref), channel_id=1, source_target_pairs={{0,384},{2,386},{4,388},{6,390},{8,392},{10,394},{12,396},{14,398}... | collective-permute-start | bytes 442376 | tf_op jit(solution)/shard_map/ppermute | solution.py:304
  83.2 4.9 %factor.1.inverse_ref = f32[128,128]{1,0:T(8,128)S(1)} custom-call(f32[96,128]{1,0:T(8,128)S(1)} %bitcast.5), custom_call_target="tpu_custom_call" | custom-call | tf_op jit(solution)/shard_map/factor/pallas_call | solution.py:151
  88.2 0.0 collective-permute-done.other_ref
  88.2 0.5 right.1
  88.7 6.0 %psum.15 = f32[8,128]{1,0:T(8,128)S(1)} all-reduce(f32[8,128]{1,0:T(8,128)S(1)} %get-tuple-element.11), channel_id=1, replica_groups=mesh['dp'=384,'tensor'=2] {'tensor'}, use_global_device_ids=true, to_apply=%region_2.3 | all-reduce | flops 1024 | bytes 8192 | tf_op jit(solution)/shard_map/psum | solution.py:308
  94.7 0.2 broadcast_in_dim.8
  94.8 0.0 copy-start.1
  94.9 22.6 %all_to_all.23.right_ref = f32[8,584,128]{2,1,0:T(8,128)S(1)} all-to-all(f32[8,584,128]{2,1,0:T(8,128)S(1)} %broadcast_in_dim.8), channel_id=1, replica_groups={{0,2,24,26,192,194,216,218},{767,745,599,577,191,169,23,1},{747,749,579..., dimensions={0} | all-to-all | bytes 4784128 | tf_op jit(solution)/shard_map/all_to_all | solution.py:278
  117.5 0.0 copy-done.1
  117.5 2.0 %update.1 = (f32[16,4608]{1,0:T(8,128)}, f32[16,4608]{1,0:T(8,128)}, f32[4608,128]{1,0:T(8,128)}) custom-call(f32[8,584,128]{2,1,0:T(8,128)S(1)} %all_to_all.23.right_ref, f32[16,128]{1,0:T(8,128)S(1)} %get-tuple-element.12.left_ref, f32[16,4608]{1,0:T(8,128)S(1)} %convert_add_fusion.buffer_ref, f32[16,4608]{1,0:T(8,128)S(1)} %copy-done.1), custom_call_target="tpu_custom_call" | custom-call | tf_op jit(solution)/shard_map/update/pallas_call | solution.py:239
  (7 shorter events, 0.1 us)
Async XLA Ops:
  1.7 1.7 %copy-start = (f32[4608,128]{1,0:T(8,128)S(1)}, f32[4608,128]{1,0:T(8,128)}, u32[]{:S(2)}) copy-start(f32[4608,128]{1,0:T(8,128)} %factor_ref.1) | copy-start | bytes 7077892
  78.8 9.4 %collective-permute-start = (f32[288,128]{1,0:T(8,128)S(1)}, f32[288,128]{1,0:T(8,128)S(1)}, u32[]{:S(2)}, u32[]{:S(2)}) collective-permute-start(f32[288,128]{1,0:T(8,128)S(1)} %reshape.23.own_ref), channel_id=1, source_target_pairs={{0,384},{2,386},{4,388},{6,390},{8,392},{10,394},{12,396},{14,398}... | collective-permute-start | bytes 442376 | tf_op jit(solution)/shard_map/ppermute | solution.py:304
  94.8 22.6 %copy-start.1 = (f32[16,4608]{1,0:T(8,128)S(1)}, f32[16,4608]{1,0:T(8,128)}, u32[]{:S(2)}) copy-start(f32[16,4608]{1,0:T(8,128)} %weight_ref.1) | copy-start | bytes 884740

commit v6 on v5

--- a/solution.py
+++ b/solution.py
@@ -19,8 +19,8 @@
 ANY = pl.BlockSpec(memory_space=pl.ANY)
 
 
-def params():
-    return pltpu.CompilerParams(vmem_limit_bytes=16 * 1024 * 1024)
+def params(limit=16 * 1024 * 1024):
+    return pltpu.CompilerParams(vmem_limit_bytes=limit)
 
 
 def split(value, parts=2):
@@ -31,18 +31,31 @@
     return out
 
 
-def head_kernel(buffer_ref, factor_ref, parts_ref, left_ref):
+def head_kernel(buffer_ref, factor_ref, parts_ref, left_ref, held, arrived):
     n_parts, rows, wide = parts_ref.shape
-    chunk = buffer_ref.shape[1] // n_parts
+    cols = buffer_ref.shape[1]
+    chunk, third = cols // n_parts, cols // 3
+    copies = [
+        pltpu.make_async_copy(
+            factor_ref.at[at : at + third, :], held.at[at : at + third, :], arrived.at[k]
+        )
+        for k, at in enumerate(range(0, cols, third))
+    ]
+    for copy in copies:
+        copy.start()
     zeros = jnp.zeros((rows, wide - chunk), jnp.float32)
     for k in range(n_parts):
         part = buffer_ref[:, k * chunk : (k + 1) * chunk]
         parts_ref[k, :, :] = jnp.concatenate([part, zeros], axis=1)
-    b1, b2 = split(buffer_ref[...])
-    f1, f2 = split(factor_ref[...])
-    both = jnp.dot(jnp.concatenate([b1, b2], axis=0), f1, preferred_element_type=jnp.float32)
-    small = both[rows:] + jnp.dot(b1, f2, preferred_element_type=jnp.float32)
-    left_ref[...] = small + both[:rows]
+    total = jnp.zeros((rows, RANK), jnp.float32)
+    for k, copy in enumerate(copies):
+        copy.wait()
+        b1, b2 = split(buffer_ref[:, k * third : (k + 1) * third])
+        f1, f2 = split(held[k * third : (k + 1) * third, :])
+        both = jnp.dot(jnp.concatenate([b1, b2], axis=0), f1, preferred_element_type=jnp.float32)
+        small = both[rows:] + jnp.dot(b1, f2, preferred_element_type=jnp.float32)
+        total = total + (small + both[:rows])
+    left_ref[...] = total
 
 
 def head(buffer, right_factor, n_parts, wide):
@@ -53,9 +66,13 @@
             jax.ShapeDtypeStruct((n_parts, rows, wide), jnp.float32),
             jax.ShapeDtypeStruct((rows, RANK), jnp.float32),
         ),
-        in_specs=[VM, VM],
+        in_specs=[VM, ANY],
         out_specs=(VM, VM),
-        compiler_params=params(),
+        scratch_shapes=[
+            pltpu.VMEM(right_factor.shape, jnp.float32),
+            pltpu.SemaphoreType.DMA((3,)),
+        ],
+        compiler_params=params(54_000_000),
         name="head",
     )(buffer, right_factor)
 

time: 120 us -> 120 us (level)
  local copies, waits for them, and re-layouts: 1.88 us -> 0.22 us
  Pallas kernels: 8.51 us -> 9.86 us
    unnamed x4 -> x2, local copies, waits for them, and re-layouts: 1.67 us -> 0.01 us
    pallas_call x1, Pallas kernels: 0.56 us -> 1.91 us  [head(): pl.pallas_call(head_kernel, out_shape=(jax.ShapeDtypeStruct((n_parts, row...]
where the time goes in v6:
time: 120 us; the launch traced here: 119 us
  blocking collectives  103 us (86%)
  Pallas kernels  9.86 us (8%)
  starting transfers between devices  4.34 us (4%)
    all_to_all x4, blocking collectives, exchange(): lax.all_to_all(blocks, ALL, 0, 0, axis_index_groups=members, tiled=True)  84.2 us
    psum x1, blocking collectives, per_device(): left_raw = lax.psum(left_part, 'tensor')  12.7 us
    psum x1, blocking collectives, per_device(): squares = lax.psum(squares, 'tensor')  5.96 us
    pallas_call x1, Pallas kernels, factor(): pl.pallas_call(factor_kernel, out_shape=jax.ShapeDtypeStruct((RANK, RANK)...  4.93 us
    ppermute x1, starting transfers between devices, per_device(): lax.ppermute(own, 'dp', [(i, (i + count // 2) % count) for i in range(cou...  4.34 us
  transfers between devices with their start and end apart: 1, of which 0 were waited for; matrix products, arithmetic and copies ran while one was open for 0% of the time, Pallas kernels for 4%

profile of v6, /device:TPU:1, one launch (start us, length us, event | category | flops | bytes accessed | tf_op | source)
XLA Modules:
  0.0 119.2 jit_solution(15502698827851472028)
XLA Ops:
  0.6 1.0 convert_add_fusion.buffer_ref
  1.7 1.9 %head.1 = (f32[16,16,384]{2,1,0:T(8,128)S(1)}, f32[16,128]{1,0:T(8,128)S(1)}) custom-call(f32[16,4608]{1,0:T(8,128)S(1)} %convert_add_fusion.buffer_ref, f32[4608,128]{1,0:T(8,128)} %factor_ref.1), custom_call_target="tpu_custom_call" | custom-call | tf_op jit(solution)/shard_map/head/pallas_call | solution.py:63
  3.6 12.7 %psum.14.left_raw_ref = f32[16,128]{1,0:T(8,128)S(1)} all-reduce(f32[16,128]{1,0:T(8,128)S(1)} %get-tuple-element.9), channel_id=1, replica_groups=mesh['dp'=384,'tensor'=2] {'tensor'}, use_global_device_ids=true, to_apply=%region_0.0 | all-reduce | flops 2048 | bytes 16384 | tf_op jit(solution)/shard_map/psum | solution.py:311
  16.3 15.9 %all_to_all.20 = f32[16,16,512]{2,1,0:T(8,128)S(1)} all-to-all(f32[16,16,512]{2,1,0:T(8,128)S(1)} %pad_maximum_fusion), channel_id=1, replica_groups={{0,384,2,386,24,408,26,410,192,576,194,578,216,600,218,602},{767,383,74..., dimensions={0} | all-to-all | bytes 1048576 | tf_op jit(solution)/shard_map/all_to_all | solution.py:295
  32.2 0.5 part.1
  32.7 25.8 %all_to_all.21 = f32[24,16,128]{2,1,0:T(8,128)S(1)} all-to-all(f32[24,16,128]{2,1,0:T(8,128)S(1)} %part.1), channel_id=1, replica_groups={{0,4,8,12,16,20,48,52,56,60,64,68,96,100,104,108,112,116,144,148,152,15..., dimensions={0} | all-to-all | bytes 393216 | tf_op jit(solution)/shard_map/all_to_all | solution.py:295
  58.6 19.9 %all_to_all.22 = f32[24,16,128]{2,1,0:T(8,128)S(1)} all-to-all(f32[24,16,128]{2,1,0:T(8,128)S(1)} %broadcast_in_dim.7), channel_id=1, replica_groups={{0,4,8,12,16,20,48,52,56,60,64,68,96,100,104,108,112,116,144,148,152,15..., dimensions={0} | all-to-all | bytes 393216 | tf_op jit(solution)/shard_map/all_to_all | solution.py:295
  78.5 4.3 %collective-permute-start = (f32[288,128]{1,0:T(8,128)S(1)}, f32[288,128]{1,0:T(8,128)S(1)}, u32[]{:S(2)}, u32[]{:S(2)}) collective-permute-start(f32[288,128]{1,0:T(8,128)S(1)} %reshape.23.own_ref), channel_id=1, source_target_pairs={{0,384},{2,386},{4,388},{6,390},{8,392},{10,394},{12,396},{14,398}... | collective-permute-start | bytes 442376 | tf_op jit(solution)/shard_map/ppermute | solution.py:321
  82.9 4.9 %factor.1.inverse_ref = f32[128,128]{1,0:T(8,128)S(1)} custom-call(f32[96,128]{1,0:T(8,128)S(1)} %bitcast.5), custom_call_target="tpu_custom_call" | custom-call | tf_op jit(solution)/shard_map/factor/pallas_call | solution.py:168
  87.9 0.0 collective-permute-done.other_ref
  87.9 0.5 right.1
  88.4 6.0 %psum.15 = f32[8,128]{1,0:T(8,128)S(1)} all-reduce(f32[8,128]{1,0:T(8,128)S(1)} %get-tuple-element.11), channel_id=1, replica_groups=mesh['dp'=384,'tensor'=2] {'tensor'}, use_global_device_ids=true, to_apply=%region_2.3 | all-reduce | flops 1024 | bytes 8192 | tf_op jit(solution)/shard_map/psum | solution.py:325
  94.4 0.2 broadcast_in_dim.8
  94.5 0.0 copy-start
  94.6 22.6 %all_to_all.23.right_ref = f32[8,584,128]{2,1,0:T(8,128)S(1)} all-to-all(f32[8,584,128]{2,1,0:T(8,128)S(1)} %broadcast_in_dim.8), channel_id=1, replica_groups={{0,2,24,26,192,194,216,218},{767,745,599,577,191,169,23,1},{747,749,579..., dimensions={0} | all-to-all | bytes 4784128 | tf_op jit(solution)/shard_map/all_to_all | solution.py:295
  117.2 0.0 copy-done
  117.2 2.0 %update.1 = (f32[16,4608]{1,0:T(8,128)}, f32[16,4608]{1,0:T(8,128)}, f32[4608,128]{1,0:T(8,128)}) custom-call(f32[8,584,128]{2,1,0:T(8,128)S(1)} %all_to_all.23.right_ref, f32[16,128]{1,0:T(8,128)S(1)} %get-tuple-element.12.left_ref, f32[16,4608]{1,0:T(8,128)S(1)} %convert_add_fusion.buffer_ref, f32[16,4608]{1,0:T(8,128)S(1)} %copy-done), custom_call_target="tpu_custom_call" | custom-call | tf_op jit(solution)/shard_map/update/pallas_call | solution.py:256
  (7 shorter events, 0.1 us)
Async XLA Ops:
  78.5 9.4 %collective-permute-start = (f32[288,128]{1,0:T(8,128)S(1)}, f32[288,128]{1,0:T(8,128)S(1)}, u32[]{:S(2)}, u32[]{:S(2)}) collective-permute-start(f32[288,128]{1,0:T(8,128)S(1)} %reshape.23.own_ref), channel_id=1, source_target_pairs={{0,384},{2,386},{4,388},{6,390},{8,392},{10,394},{12,396},{14,398}... | collective-permute-start | bytes 442376 | tf_op jit(solution)/shard_map/ppermute | solution.py:321
  94.5 22.6 %copy-start = (f32[16,4608]{1,0:T(8,128)S(1)}, f32[16,4608]{1,0:T(8,128)}, u32[]{:S(2)}) copy-start(f32[16,4608]{1,0:T(8,128)} %weight_ref.1) | copy-start | bytes 884740

commit v7 on v6

--- a/solution.py
+++ b/solution.py
@@ -211,10 +211,10 @@
     weight_new, momentum_new, factor_new, sent,
 ):
     near, pitch, _ = right_ref.shape
-    chunk, group = pitch - 8, 2
-    squares = right_ref[0, chunk:, :]
+    chunk, group = (pitch - 8) // 2, 4
+    squares = right_ref[0, 2 * chunk :, :]
     for k in range(1, near):
-        squares = squares + right_ref[k, chunk:, :]
+        squares = squares + right_ref[k, 2 * chunk :, :]
     scale = lax.rsqrt(jnp.sum(squares, axis=0, keepdims=True) + 1e-06)
     left = left_ref[...]
     high, low = split(jnp.concatenate([decay * left, (gain * left) * scale], axis=0))
@@ -232,14 +232,20 @@
         copies.append(pltpu.make_async_copy(source, target, sent.at[len(copies)]))
         copies[-1].start()
 
-    for first in range(0, near, group):
-        for k in range(first, first + group):
-            factor_new[k * chunk : (k + 1) * chunk, :] = right_ref[k, :chunk, :] * scale
-        at, end = first * chunk, (first + group) * chunk
+    blocks = [(half, first) for half in range(2) for first in range(0, near, group)]
+    for half, first in blocks:
+        at = (half * near + first) * chunk
+        end = at + group * chunk
+        for k in range(group):
+            rows = right_ref[first + k, half * chunk : (half + 1) * chunk, :]
+            factor_new[at + k * chunk : at + (k + 1) * chunk, :] = rows * scale
         send(factor_new.at[at:end, :], factor_out.at[at:end, :])
-    for first in range(0, near, group):
-        at, end = first * chunk, (first + group) * chunk
-        right = jnp.concatenate([right_ref[first + k, :chunk, :] for k in range(group)], axis=0)
+    for half, first in blocks:
+        at = (half * near + first) * chunk
+        end = at + group * chunk
+        right = jnp.concatenate(
+            [right_ref[first + k, half * chunk : (half + 1) * chunk, :] for k in range(group)], axis=0
+        )
         both = jnp.concatenate(split(right), axis=1)
         out = lax.dot_general(both_left, both, NT, preferred_element_type=jnp.float32)
         out = out[: 2 * n] + out[2 * n :]
@@ -283,11 +289,11 @@
 
 
 def far(x, y, z):
-    return y // 2, z // 2
+    return z // 2, y // 2
 
 
 CUBE = groups(lambda x, y, z: (x // 2, y // 2, z // 2), cube)
-NEAR = groups(far, lambda x, y, z: cube(x, y, z) + (x // 2,))
+NEAR = groups(far, lambda x, y, z: (x // 2,) + cube(x, y, z))
 FAR = groups(lambda x, y, z: cube(x, y, z) + (x // 2,), far)
 
 

time: 120 us -> 121 us (level)
  blocking collectives: 103 us -> 106 us
  starting transfers between devices: 4.34 us -> 1.92 us
    all_to_all x4, blocking collectives: 84.2 us -> 87.3 us  [exchange(): lax.all_to_all(blocks, ALL, 0, 0, axis_index_groups=members, tiled=True)]
    ppermute x1, starting transfers between devices: 4.34 us -> 1.92 us  [per_device(): lax.ppermute(own, 'dp', [(i, (i + count // 2) % count) for i in range(cou...]
  transfers between devices with their start and end apart: 1 -> 1, of which waited for: 0 -> 1; matrix products, arithmetic and copies ran while one was open for 0% -> 0% of each run, Pallas kernels for 4% -> 4%
where the time goes in v7:
time: 121 us; the launch traced here: 120 us
  blocking collectives  106 us (88%)
  Pallas kernels  9.85 us (8%)
  starting transfers between devices  1.92 us (2%)
    all_to_all x4, blocking collectives, exchange(): lax.all_to_all(blocks, ALL, 0, 0, axis_index_groups=members, tiled=True)  87.3 us
    psum x1, blocking collectives, per_device(): left_raw = lax.psum(left_part, 'tensor')  12.7 us
    psum x1, blocking collectives, per_device(): squares = lax.psum(squares, 'tensor')  6.21 us
    pallas_call x1, Pallas kernels, factor(): pl.pallas_call(factor_kernel, out_shape=jax.ShapeDtypeStruct((RANK, RANK)...  4.93 us
  transfers between devices with their start and end apart: 1, of which 1 were waited for; matrix products, arithmetic and copies ran while one was open for 0% of the time, Pallas kernels for 4%

profile of v7, /device:TPU:1, one launch (start us, length us, event | category | flops | bytes accessed | tf_op | source)
XLA Modules:
  0.0 120.5 jit_solution(9687338773036236729)
XLA Ops:
  0.6 1.0 convert_add_fusion.buffer_ref
  1.7 1.9 %head.1 = (f32[16,16,384]{2,1,0:T(8,128)S(1)}, f32[16,128]{1,0:T(8,128)S(1)}) custom-call(f32[16,4608]{1,0:T(8,128)S(1)} %convert_add_fusion.buffer_ref, f32[4608,128]{1,0:T(8,128)} %factor_ref.1), custom_call_target="tpu_custom_call" | custom-call | tf_op jit(solution)/shard_map/head/pallas_call | solution.py:63
  3.6 12.7 %psum.14.left_raw_ref = f32[16,128]{1,0:T(8,128)S(1)} all-reduce(f32[16,128]{1,0:T(8,128)S(1)} %get-tuple-element.9), channel_id=1, replica_groups=mesh['dp'=384,'tensor'=2] {'tensor'}, use_global_device_ids=true, to_apply=%region_0.0 | all-reduce | flops 2048 | bytes 16384 | tf_op jit(solution)/shard_map/psum | solution.py:317
  16.3 16.1 %all_to_all.20 = f32[16,16,512]{2,1,0:T(8,128)S(1)} all-to-all(f32[16,16,512]{2,1,0:T(8,128)S(1)} %pad_maximum_fusion), channel_id=1, replica_groups={{0,2,24,26,192,194,216,218,384,386,408,410,576,578,600,602},{767,745,59..., dimensions={0} | all-to-all | bytes 1048576 | tf_op jit(solution)/shard_map/all_to_all | solution.py:301
  32.5 0.5 part.1
  33.0 28.4 %all_to_all.21 = f32[24,16,128]{2,1,0:T(8,128)S(1)} all-to-all(f32[24,16,128]{2,1,0:T(8,128)S(1)} %part.1), channel_id=1, replica_groups={{0,48,96,144,4,52,100,148,8,56,104,152,12,60,108,156,16,64,112,160,20,6..., dimensions={0} | all-to-all | bytes 393216 | tf_op jit(solution)/shard_map/all_to_all | solution.py:301
  61.4 20.4 %all_to_all.22 = f32[24,16,128]{2,1,0:T(8,128)S(1)} all-to-all(f32[24,16,128]{2,1,0:T(8,128)S(1)} %broadcast_in_dim.7), channel_id=1, replica_groups={{0,48,96,144,4,52,100,148,8,56,104,152,12,60,108,156,16,64,112,160,20,6..., dimensions={0} | all-to-all | bytes 393216 | tf_op jit(solution)/shard_map/all_to_all | solution.py:301
  81.8 1.9 %collective-permute-start = (f32[288,128]{1,0:T(8,128)S(1)}, f32[288,128]{1,0:T(8,128)S(1)}, u32[]{:S(2)}, u32[]{:S(2)}) collective-permute-start(f32[288,128]{1,0:T(8,128)S(1)} %reshape.23.own_ref), channel_id=1, source_target_pairs={{0,384},{2,386},{4,388},{6,390},{8,392},{10,394},{12,396},{14,398}... | collective-permute-start | bytes 442376 | tf_op jit(solution)/shard_map/ppermute | solution.py:327
  83.8 4.9 %factor.1.inverse_ref = f32[128,128]{1,0:T(8,128)S(1)} custom-call(f32[96,128]{1,0:T(8,128)S(1)} %bitcast.5), custom_call_target="tpu_custom_call" | custom-call | tf_op jit(solution)/shard_map/factor/pallas_call | solution.py:168
  88.8 0.4 collective-permute-done.other_ref
  89.2 0.5 right.1
  89.7 6.2 %psum.15 = f32[8,128]{1,0:T(8,128)S(1)} all-reduce(f32[8,128]{1,0:T(8,128)S(1)} %get-tuple-element.11), channel_id=1, replica_groups=mesh['dp'=384,'tensor'=2] {'tensor'}, use_global_device_ids=true, to_apply=%region_2.3 | all-reduce | flops 1024 | bytes 8192 | tf_op jit(solution)/shard_map/psum | solution.py:331
  95.9 0.2 broadcast_in_dim.8
  96.1 0.0 copy-start
  96.1 22.4 %all_to_all.23.right_ref = f32[8,584,128]{2,1,0:T(8,128)S(1)} all-to-all(f32[8,584,128]{2,1,0:T(8,128)S(1)} %broadcast_in_dim.8), channel_id=1, replica_groups={{0,2,24,26,192,194,216,218},{767,745,599,577,191,169,23,1},{747,749,579..., dimensions={0} | all-to-all | bytes 4784128 | tf_op jit(solution)/shard_map/all_to_all | solution.py:301
  118.5 0.0 copy-done
  118.5 2.0 %update.1 = (f32[16,4608]{1,0:T(8,128)}, f32[16,4608]{1,0:T(8,128)}, f32[4608,128]{1,0:T(8,128)}) custom-call(f32[8,584,128]{2,1,0:T(8,128)S(1)} %all_to_all.23.right_ref, f32[16,128]{1,0:T(8,128)S(1)} %get-tuple-element.12.left_ref, f32[16,4608]{1,0:T(8,128)S(1)} %convert_add_fusion.buffer_ref, f32[16,4608]{1,0:T(8,128)S(1)} %copy-done), custom_call_target="tpu_custom_call" | custom-call | tf_op jit(solution)/shard_map/update/pallas_call | solution.py:262
  (7 shorter events, 0.1 us)
Async XLA Ops:
  81.8 7.4 %collective-permute-start = (f32[288,128]{1,0:T(8,128)S(1)}, f32[288,128]{1,0:T(8,128)S(1)}, u32[]{:S(2)}, u32[]{:S(2)}) collective-permute-start(f32[288,128]{1,0:T(8,128)S(1)} %reshape.23.own_ref), channel_id=1, source_target_pairs={{0,384},{2,386},{4,388},{6,390},{8,392},{10,394},{12,396},{14,398}... | collective-permute-start | bytes 442376 | tf_op jit(solution)/shard_map/ppermute | solution.py:327
  96.1 22.4 %copy-start = (f32[16,4608]{1,0:T(8,128)S(1)}, f32[16,4608]{1,0:T(8,128)}, u32[]{:S(2)}) copy-start(f32[16,4608]{1,0:T(8,128)} %weight_ref.1) | copy-start | bytes 884740

commit v8 on v7

--- a/solution.py
+++ b/solution.py
@@ -289,7 +289,7 @@
 
 
 def far(x, y, z):
-    return z // 2, y // 2
+    return y // 2, z // 2
 
 
 CUBE = groups(lambda x, y, z: (x // 2, y // 2, z // 2), cube)

time: 121 us -> 120 us (level)
  blocking collectives: 106 us -> 104 us
  starting transfers between devices: 1.92 us -> 3.45 us
    all_to_all x4, blocking collectives: 87.3 us -> 84.7 us  [exchange(): lax.all_to_all(blocks, ALL, 0, 0, axis_index_groups=members, tiled=True)]
    ppermute x1, starting transfers between devices: 1.92 us -> 3.45 us  [per_device(): lax.ppermute(own, 'dp', [(i, (i + count // 2) % count) for i in range(cou...]
  transfers between devices with their start and end apart: 1 -> 1, of which waited for: 1 -> 0; matrix products, arithmetic and copies ran while one was open for 0% -> 0% of each run, Pallas kernels for 4% -> 4%
where the time goes in v8:
time: 120 us; the launch traced here: 119 us
  blocking collectives  104 us (87%)
  Pallas kernels  9.85 us (8%)
  starting transfers between devices  3.45 us (3%)
    all_to_all x4, blocking collectives, exchange(): lax.all_to_all(blocks, ALL, 0, 0, axis_index_groups=members, tiled=True)  84.7 us
    psum x1, blocking collectives, per_device(): left_raw = lax.psum(left_part, 'tensor')  12.7 us
    psum x1, blocking collectives, per_device(): squares = lax.psum(squares, 'tensor')  6.6 us
    pallas_call x1, Pallas kernels, factor(): pl.pallas_call(factor_kernel, out_shape=jax.ShapeDtypeStruct((RANK, RANK)...  4.93 us
    ppermute x1, starting transfers between devices, per_device(): lax.ppermute(own, 'dp', [(i, (i + count // 2) % count) for i in range(cou...  3.45 us
  transfers between devices with their start and end apart: 1, of which 0 were waited for; matrix products, arithmetic and copies ran while one was open for 0% of the time, Pallas kernels for 4%

profile of v8, /device:TPU:1, one launch (start us, length us, event | category | flops | bytes accessed | tf_op | source)
XLA Modules:
  0.0 119.4 jit_solution(15488427770757688647)
XLA Ops:
  0.6 1.0 convert_add_fusion.buffer_ref
  1.7 1.9 %head.1 = (f32[16,16,384]{2,1,0:T(8,128)S(1)}, f32[16,128]{1,0:T(8,128)S(1)}) custom-call(f32[16,4608]{1,0:T(8,128)S(1)} %convert_add_fusion.buffer_ref, f32[4608,128]{1,0:T(8,128)} %factor_ref.1), custom_call_target="tpu_custom_call" | custom-call | tf_op jit(solution)/shard_map/head/pallas_call | solution.py:63
  3.6 12.7 %psum.14.left_raw_ref = f32[16,128]{1,0:T(8,128)S(1)} all-reduce(f32[16,128]{1,0:T(8,128)S(1)} %get-tuple-element.9), channel_id=1, replica_groups=mesh['dp'=384,'tensor'=2] {'tensor'}, use_global_device_ids=true, to_apply=%region_0.0 | all-reduce | flops 2048 | bytes 16384 | tf_op jit(solution)/shard_map/psum | solution.py:317
  16.3 16.1 %all_to_all.20 = f32[16,16,512]{2,1,0:T(8,128)S(1)} all-to-all(f32[16,16,512]{2,1,0:T(8,128)S(1)} %pad_maximum_fusion), channel_id=1, replica_groups={{0,2,24,26,192,194,216,218,384,386,408,410,576,578,600,602},{767,745,59..., dimensions={0} | all-to-all | bytes 1048576 | tf_op jit(solution)/shard_map/all_to_all | solution.py:301
  32.5 0.5 part.1
  33.0 25.8 %all_to_all.21 = f32[24,16,128]{2,1,0:T(8,128)S(1)} all-to-all(f32[24,16,128]{2,1,0:T(8,128)S(1)} %part.1), channel_id=1, replica_groups={{0,4,8,12,16,20,48,52,56,60,64,68,96,100,104,108,112,116,144,148,152,15..., dimensions={0} | all-to-all | bytes 393216 | tf_op jit(solution)/shard_map/all_to_all | solution.py:301
  58.8 20.0 %all_to_all.22 = f32[24,16,128]{2,1,0:T(8,128)S(1)} all-to-all(f32[24,16,128]{2,1,0:T(8,128)S(1)} %broadcast_in_dim.7), channel_id=1, replica_groups={{0,4,8,12,16,20,48,52,56,60,64,68,96,100,104,108,112,116,144,148,152,15..., dimensions={0} | all-to-all | bytes 393216 | tf_op jit(solution)/shard_map/all_to_all | solution.py:301
  78.9 3.5 %collective-permute-start = (f32[288,128]{1,0:T(8,128)S(1)}, f32[288,128]{1,0:T(8,128)S(1)}, u32[]{:S(2)}, u32[]{:S(2)}) collective-permute-start(f32[288,128]{1,0:T(8,128)S(1)} %reshape.23.own_ref), channel_id=1, source_target_pairs={{0,384},{2,386},{4,388},{6,390},{8,392},{10,394},{12,396},{14,398}... | collective-permute-start | bytes 442376 | tf_op jit(solution)/shard_map/ppermute | solution.py:327
  82.4 4.9 %factor.1.inverse_ref = f32[128,128]{1,0:T(8,128)S(1)} custom-call(f32[96,128]{1,0:T(8,128)S(1)} %bitcast.5), custom_call_target="tpu_custom_call" | custom-call | tf_op jit(solution)/shard_map/factor/pallas_call | solution.py:168
  87.4 0.0 collective-permute-done.other_ref
  87.4 0.5 right.1
  87.9 6.6 %psum.15 = f32[8,128]{1,0:T(8,128)S(1)} all-reduce(f32[8,128]{1,0:T(8,128)S(1)} %get-tuple-element.11), channel_id=1, replica_groups=mesh['dp'=384,'tensor'=2] {'tensor'}, use_global_device_ids=true, to_apply=%region_2.3 | all-reduce | flops 1024 | bytes 8192 | tf_op jit(solution)/shard_map/psum | solution.py:331
  94.5 0.2 broadcast_in_dim.8
  94.7 0.0 copy-start
  94.7 22.7 %all_to_all.23.right_ref = f32[8,584,128]{2,1,0:T(8,128)S(1)} all-to-all(f32[8,584,128]{2,1,0:T(8,128)S(1)} %broadcast_in_dim.8), channel_id=1, replica_groups={{0,2,24,26,192,194,216,218},{767,745,599,577,191,169,23,1},{747,749,579..., dimensions={0} | all-to-all | bytes 4784128 | tf_op jit(solution)/shard_map/all_to_all | solution.py:301
  117.4 0.0 copy-done
  117.4 2.0 %update.1 = (f32[16,4608]{1,0:T(8,128)}, f32[16,4608]{1,0:T(8,128)}, f32[4608,128]{1,0:T(8,128)}) custom-call(f32[8,584,128]{2,1,0:T(8,128)S(1)} %all_to_all.23.right_ref, f32[16,128]{1,0:T(8,128)S(1)} %get-tuple-element.12.left_ref, f32[16,4608]{1,0:T(8,128)S(1)} %convert_add_fusion.buffer_ref, f32[16,4608]{1,0:T(8,128)S(1)} %copy-done), custom_call_target="tpu_custom_call" | custom-call | tf_op jit(solution)/shard_map/update/pallas_call | solution.py:262
  (7 shorter events, 0.1 us)
Async XLA Ops:
  78.9 8.5 %collective-permute-start = (f32[288,128]{1,0:T(8,128)S(1)}, f32[288,128]{1,0:T(8,128)S(1)}, u32[]{:S(2)}, u32[]{:S(2)}) collective-permute-start(f32[288,128]{1,0:T(8,128)S(1)} %reshape.23.own_ref), channel_id=1, source_target_pairs={{0,384},{2,386},{4,388},{6,390},{8,392},{10,394},{12,396},{14,398}... | collective-permute-start | bytes 442376 | tf_op jit(solution)/shard_map/ppermute | solution.py:327
  94.7 22.7 %copy-start = (f32[16,4608]{1,0:T(8,128)S(1)}, f32[16,4608]{1,0:T(8,128)}, u32[]{:S(2)}) copy-start(f32[16,4608]{1,0:T(8,128)} %weight_ref.1) | copy-start | bytes 884740
